TPU v7x, 256 devices: a whole 4x4x8 slice. The times are simulated.
256 devices in a mesh: dens: 8 (over z_hi, core), sp: 32 (over y, z_lo, x).
Axes of the slice: x: 4, y: 4, z: 8 (z_hi: 4, z_lo: 2; z = z_hi * 2 + z_lo), core: 2. Of those that a mesh axis runs over, the one named last changes fastest.
Arguments:
- densities: float32 [8, 64, 512, 512], P('dens', 'sp'), may hold values from 0.2 to 5
- weights: float32 [8], P('dens'), may hold values from 0.5 to 2
- spreads: float32 [3], replicated, may hold values from 1 to 3.2, as said below
Outputs:
- barycenter: float32 [64, 512, 512], P('sp')
- scalings: float32 [8, 64, 512, 512], P('dens', 'sp')
Inputs may be any that keep to these rules, and one draw needn't show every extreme that they name: The vertical width spreads[0] lies within 2.4 to 3.2 cells, the two horizontal widths within 1.0 to 2.5 cells.
All inputs are finite; a program needn't handle non-finite values.
Results may differ from a plain program's by a relative error of at most 0.0001.
Values sent between devices are 32-bit elements; how exact they have to be, the bound alone decides.
A program may use at most 64 MiB of HBM per device.

v0:
```python
import jax
import jax.numpy as jnp
from jax import lax
from jax.sharding import PartitionSpec as P

ITERS = 2


def kernel_matrix(length, spread):
    pos = jnp.arange(length).astype(jnp.float32)
    diff = (pos[:, None] - pos[None, :]) / spread
    return jnp.exp(-diff * diff) / (spread * jnp.sqrt(jnp.float32(jnp.pi)))


def along_planes(field, kern_x, kern_y):
    hp = lax.Precision.HIGHEST
    field = jnp.einsum("zxy,yk->zxk", field, kern_y, precision=hp)
    return jnp.einsum("zxy,xk->zky", field, kern_x, precision=hp)


def along_columns(field, kern_z):
    return jnp.einsum("zxy,zk->kxy", field, kern_z, precision=lax.Precision.HIGHEST)


def to_columns(field):
    return lax.all_to_all(field, "sp", split_axis=1, concat_axis=0, tiled=True)


def to_planes(field):
    return lax.all_to_all(field, "sp", split_axis=0, concat_axis=1, tiled=True)


def local(densities, weights, spreads):
    nz = densities.shape[1] * lax.axis_size("sp")
    nx = densities.shape[2]
    ny = densities.shape[3]
    kern_z = kernel_matrix(nz, spreads[0])
    kern_x = kernel_matrix(nx, spreads[1])
    kern_y = kernel_matrix(ny, spreads[2])
    total_weight = lax.psum(weights[0], "dens")
    own_weight = weights[0]
    target = densities[0]
    scale_v = jnp.ones_like(target)
    barycenter = scale_v

    def convolve(field):
        planar = along_planes(field, kern_x, kern_y)
        columns = along_columns(to_columns(planar), kern_z)
        return to_planes(columns)

    scale_w = scale_v
    for step in range(ITERS):
        scale_w = target / convolve(scale_v)
        marginal = scale_v * convolve(scale_w)
        term = own_weight * jnp.log(marginal)
        summed = lax.psum(term, "dens")
        barycenter = jnp.exp(summed / total_weight)
        scale_v = scale_v * barycenter / marginal
    return (barycenter, scale_w[None])


def solution(mesh):
    return jax.shard_map(
        local,
        mesh=mesh,
        in_specs=(P("dens", "sp", None, None), P("dens"), P()),
        out_specs=(P("sp", None, None), P("dens", "sp", None, None)),
        check_vma=False,
    )
```

profile of v0, /device:TPU:1, one launch (start us, length us, event | category | flops | bytes accessed | tf_op | source)
XLA Modules:
  0.0 560.1 jit_solution(9381888227329281751)
XLA Ops:
  9.9 4.4 fusion.19
  14.3 4.3 convolution_bitcast_fusion.3
  21.6 9.4 %all-to-all-start = ((f32[2,512,512]{2,0,1:T(2,128)}), f32[2,512,512]{2,0,1:T(2,128)S(1)}, u32[]{:S(2)}, u32[]{:S(2)}) async-start(f32[2,512,512]{2,0,1:T(2,128)} %copy.14), calls=%async_computation | async-start | bytes 4194304 | tf_op jit(solution)/shard_map/all_to_all | solution.py:26
  31.7 26.5 %all-to-all-done = f32[2,512,512]{2,0,1:T(2,128)S(1)} async-done(((f32[2,512,512]{2,0,1:T(2,128)}), f32[2,512,512]{2,0,1:T(2,128)S(1)}, u32[]{:S(2)}, u32[]{:S(2)}) %all-to-all-start) | async-done | bytes 2097184 | tf_op jit(solution)/shard_map/all_to_all | solution.py:26
  67.0 32.5 %all_to_all.147 = f32[64,16,512]{2,1,0:T(8,128)S(1)} all-to-all(f32[64,16,512]{2,1,0:T(8,128)S(1)} %copy.16), channel_id=1, replica_groups=mesh['dens'=8,'sp'=32] {'sp'}, dimensions={0} | all-to-all | bytes 4194304 | tf_op jit(solution)/shard_map/all_to_all | solution.py:30
  101.6 4.4 fusion.17
  106.0 4.3 convolution_bitcast_fusion.2
  112.0 33.4 %all_to_all.148 = f32[2,512,512]{2,0,1:T(2,128)S(1)} all-to-all(f32[2,512,512]{2,0,1:T(2,128)S(1)} %copy.18), channel_id=1, replica_groups=mesh['dens'=8,'sp'=32] {'sp'}, dimensions={1} | all-to-all | bytes 4194304 | tf_op jit(solution)/shard_map/all_to_all | solution.py:26
  151.4 4.1 fusion.61
  158.1 7.0 %all-to-all-start.3 = ((f32[64,16,512]{2,1,0:T(8,128)}), f32[64,16,512]{2,1,0:T(8,128)}, u32[]{:S(2)}, u32[]{:S(2)}) async-start(f32[64,16,512]{2,1,0:T(8,128)} %copy.20), calls=%async_computation.3 | async-start | bytes 4194304 | tf_op jit(solution)/shard_map/all_to_all | solution.py:30
  165.8 25.9 %all-to-all-done.3 = f32[64,16,512]{2,1,0:T(8,128)} async-done(((f32[64,16,512]{2,1,0:T(8,128)}), f32[64,16,512]{2,1,0:T(8,128)}, u32[]{:S(2)}, u32[]{:S(2)}) %all-to-all-start.3) | async-done | bytes 2097184 | tf_op jit(solution)/shard_map/all_to_all | solution.py:30
  196.6 19.9 %psum.22 = f32[]{:T(128)} all-reduce(f32[]{:T(128)} %bitcast), channel_id=1, replica_groups=mesh['dens'=8,'sp'=32] {'dens'}, use_global_device_ids=true, to_apply=%region_1.0 | all-reduce | flops 1 | bytes 8 | tf_op jit(solution)/shard_map/psum | solution.py:40
  216.4 67.1 %all-reduce.3.cloned.1.call-done = f32[2,512,512]{2,1,0:T(8,128)} async-done(((f32[2,512,512]{2,1,0:T(8,128)}), f32[2,512,512]{2,1,0:T(8,128)}) %all-reduce.3.cloned.1.call-update) | async-done | bytes 2097168 | tf_op jit(solution)/shard_map/psum | solution.py:56
  286.9 4.4 fusion.15
  291.3 4.3 convolution_bitcast_fusion.1
  297.3 33.9 %all_to_all.149 = f32[2,512,512]{2,0,1:T(2,128)S(1)} all-to-all(f32[2,512,512]{2,0,1:T(2,128)S(1)} %copy.22), channel_id=1, replica_groups=mesh['dens'=8,'sp'=32] {'sp'}, dimensions={1} | all-to-all | bytes 4194304 | tf_op jit(solution)/shard_map/all_to_all | solution.py:26
  337.4 4.1 fusion.59
  342.7 33.1 %all_to_all.150 = f32[64,16,512]{2,1,0:T(8,128)S(1)} all-to-all(f32[64,16,512]{2,1,0:T(8,128)S(1)} %copy.24), channel_id=1, replica_groups=mesh['dens'=8,'sp'=32] {'sp'}, dimensions={0} | all-to-all | bytes 4194304 | tf_op jit(solution)/shard_map/all_to_all | solution.py:30
  377.4 4.4 fusion.13
  381.8 4.3 convolution_bitcast_fusion
  387.8 32.3 %all_to_all.151 = f32[2,512,512]{2,0,1:T(2,128)S(1)} all-to-all(f32[2,512,512]{2,0,1:T(2,128)S(1)} %copy.26), channel_id=1, replica_groups=mesh['dens'=8,'sp'=32] {'sp'}, dimensions={1} | all-to-all | bytes 4194304 | tf_op jit(solution)/shard_map/all_to_all | solution.py:26
  426.2 4.1 fusion.57
  431.6 33.1 %all_to_all.152 = f32[64,16,512]{2,1,0:T(8,128)S(1)} all-to-all(f32[64,16,512]{2,1,0:T(8,128)S(1)} %copy.28), channel_id=1, replica_groups=mesh['dens'=8,'sp'=32] {'sp'}, dimensions={0} | all-to-all | bytes 4194304 | tf_op jit(solution)/shard_map/all_to_all | solution.py:30
  471.5 77.5 %all-reduce.5.cloned.1.call-done = f32[2,512,512]{2,1,0:T(8,128)} async-done(((f32[2,512,512]{2,1,0:T(8,128)}), f32[2,512,512]{2,1,0:T(8,128)}) %all-reduce.5.cloned.1.call-update) | async-done | bytes 2097168 | tf_op jit(solution)/shard_map/psum | solution.py:56
  (45 shorter events, 63.7 us)
Async XLA Ops:
  21.6 36.5 %all-to-all-start = ((f32[2,512,512]{2,0,1:T(2,128)}), f32[2,512,512]{2,0,1:T(2,128)S(1)}, u32[]{:S(2)}, u32[]{:S(2)}) async-start(f32[2,512,512]{2,0,1:T(2,128)} %copy.14), calls=%async_computation | async-start | bytes 4194304 | tf_op jit(solution)/shard_map/all_to_all | solution.py:26
  99.5 1.6 copy-start
  158.1 33.6 %all-to-all-start.3 = ((f32[64,16,512]{2,1,0:T(8,128)}), f32[64,16,512]{2,1,0:T(8,128)}, u32[]{:S(2)}, u32[]{:S(2)}) async-start(f32[64,16,512]{2,1,0:T(8,128)} %copy.20), calls=%async_computation.3 | async-start | bytes 4194304 | tf_op jit(solution)/shard_map/all_to_all | solution.py:30
  165.1 118.4 %all-reduce.3.cloned.1.call-start = ((), (), s32[]{:S(2)}) async-start(), calls=%async_computation.8 | async-start | bytes 4194304 | tf_op jit(solution)/shard_map/psum | solution.py:56
  193.6 1.3 copy-start.2
  196.5 352.5 %all-reduce.5.cloned.1.call-start = ((), (), s32[]{:S(2)}) async-start(), calls=%async_computation.9 | async-start | bytes 4194304 | tf_op jit(solution)/shard_map/psum | solution.py:56
  286.9 4.5 copy-start.3
  376.0 1.4 copy-start.1
  464.7 1.6 copy-start.4
Sparse Core Ops, SparseCore 0:
  196.6 86.8 all-reduce.2
  468.2 80.7 all-reduce.4
where the time goes:
time: 568 us; the launch traced here: 560 us
  blocking collectives  218 us (38%)
  waiting for transfers between devices  197 us (35%)
  matrix products  50 us (9%)
  local copies, waits for them, and re-layouts  46.1 us (8%)
  between operations  17.3 us (3%)
  starting transfers between devices  16.5 us (3%)
  other arithmetic  14.9 us (3%)
    psum x2, waiting for transfers between devices, local(): summed = lax.psum(term, 'dens')  145 us
    all_to_all x3, blocking collectives, to_columns(): return lax.all_to_all(field, 'sp', split_axis=1, concat_axis=0, tiled=True)  99.6 us
    all_to_all x3, blocking collectives, to_planes(): return lax.all_to_all(field, 'sp', split_axis=0, concat_axis=1, tiled=True)  98.7 us
    all_to_all x1, waiting for transfers between devices, to_columns(): return lax.all_to_all(field, 'sp', split_axis=1, concat_axis=0, tiled=True)  26.5 us
    all_to_all x1, waiting for transfers between devices, to_planes(): return lax.all_to_all(field, 'sp', split_axis=0, concat_axis=1, tiled=True)  25.9 us
    all_to_all x8, local copies, waits for them, and re-layouts, to_columns(): return lax.all_to_all(field, 'sp', split_axis=1, concat_axis=0, tiled=True)  23.4 us
    psum x1, blocking collectives, local(): total_weight = lax.psum(weights[0], 'dens')  19.9 us
    dot_general x4, matrix products, along_planes(): field = jnp.einsum('zxy,yk->zxk', field, kern_y, precision=hp)  17.7 us
  transfers between devices with their start and end apart: 4, of which 4 were waited for; matrix products, arithmetic and copies ran while one was open for 1% of the time, Pallas kernels for 0%

commit v1 on v0

v1 whole, which is shorter than its diff:
```python
import functools
import math

import jax
import jax.numpy as jnp
from jax import lax
from jax.experimental import pallas as pl
from jax.experimental.pallas import tpu as pltpu
from jax.sharding import PartitionSpec as P

MESH = pl.DeviceIdType.MESH
BF = jnp.bfloat16
F32 = jnp.float32

NXD, NYD, NZD, NHD = 4, 4, 2, 4
CH = 4
SIZE = {"x": NXD, "y": NYD, "z": NZD}
AXES = (("z", "x", "y"), ("z", "x", "y"), ("z", "x", "y"))


def order():
    steps = []
    steps += [("conv", 0, 0), ("conv", 0, 1)]
    flow = [("adv", 0, 0), ("adv", 0, 1), ("zf", 0), ("cs", 0), ("rs1", 0), ("rs2", 0), ("ag1", 0), ("ag2", 0), ("zb", 0), ("adv", 1, 0), ("adv", 1, 1)]
    when = [6.5, 13, 20, 22.5, 26, 30.5, 35, 38.5, 41, 47, 53.5]
    lag = [5, 5, 4, 4, 4.5, 5, 5.5, 5.5, 5.5, 5.5, 5.5]
    timed = []
    for c in range(CH):
        for i, step in enumerate(flow):
            timed.append((when[i] + c * lag[i], i, step + (c,)))
    steps += [t[2] for t in sorted(timed)]
    steps += [("xb", 0), ("xb", 1), ("yb",)]
    steps += [("conv", 2, 0), ("conv", 2, 1)]
    flow = [("adv", 2, 0), ("adv", 2, 1), ("zf", 2), ("cs", 2), ("rs1", 2), ("rs2", 2)]
    timed = []
    for c in range(CH):
        for i, step in enumerate(flow):
            timed.append((when[i] + c * lag[i], i, step + (c,)))
    steps += [t[2] for t in sorted(timed)]
    steps += [("tail",)]
    return steps


def split(x):
    hi = x.astype(BF)
    return hi, (x - hi.astype(F32)).astype(BF)


def dot(a, b):
    return jnp.dot(a, b, preferred_element_type=F32)


def body(
    dens_ref, wt_ref, spread_ref, bary_ref, w_ref,
    b0, b1, b2, d_ref, t_ref, cb_ref, u_ref, r1_ref, r2_ref, bar_ref, oth_ref,
    share_ref, gath_ref, whi, wlo, thi, tlo, gxh, gxl, gyh, gyl, gz3, wts, send_sem, recv_sem,
):
    dens = lax.axis_index("dens")
    sp = lax.axis_index("sp")
    zh, core = dens // 2, lax.rem(dens, 2)
    me = {"y": sp // 8, "z": lax.rem(sp // 4, 2), "x": lax.rem(sp, 4)}

    def device(h=zh, k=core, **at):
        at = {**me, **at}
        return {"dens": h * 2 + k, "sp": (at["y"] * 2 + at["z"]) * 4 + at["x"]}

    def around(axis, k):
        return lax.rem(me[axis] + k, SIZE[axis])

    right, left = lax.rem(zh + 1, 4), lax.rem(zh + 3, 4)
    far = lax.rem(zh + 2, 4)
    peers = [device(**{axis: around(axis, k)}) for axis in "xyz" for k in range(1, SIZE[axis])]
    peers += [device(k=1 - core), device(h=right), device(h=left), device(h=far)]

    barrier = pltpu.get_barrier_semaphore()
    for peer in peers:
        pl.semaphore_signal(barrier, 1, device_id=peer, device_id_type=MESH)

    root = math.sqrt(math.pi)

    def gauss(i, j, s):
        diff = (i.astype(F32) - j.astype(F32)) / s
        return jnp.exp(-diff * diff) / (s * jnp.float32(root))

    def wide(hi_ref, lo_ref, s):
        def tile(m, carry):
            at = pl.multiple_of(m * 128, 128)
            i = lax.broadcasted_iota(jnp.int32, (128, 512), 0) + at
            j = lax.broadcasted_iota(jnp.int32, (128, 512), 1)
            hi, lo = split(gauss(i, j, s))
            hi_ref[pl.ds(at, 128), :] = hi
            lo_ref[pl.ds(at, 128), :] = lo
            return carry
        lax.fori_loop(0, 4, tile, 0)

    wide(gxh, gxl, spread_ref[1])
    wide(gyh, gyl, spread_ref[2])

    def plane(q):
        return ((q >> 3) & 3) * 16 + ((q >> 2) & 1) * 8 + (q & 3) * 2 + (q >> 5)

    i = lax.broadcasted_iota(jnp.int32, (64, 192), 0)
    j = lax.broadcasted_iota(jnp.int32, (64, 192), 1)
    hi, lo = split(gauss(plane(i), plane(j & 63), spread_ref[0]))
    gz3[...] = jnp.where(j < 128, hi.astype(F32), lo.astype(F32)).astype(BF)

    def line(n, s, at, axis):
        shape = (at.shape[0], n) if axis == 1 else (n, at.shape[1])
        other = lax.broadcasted_iota(jnp.int32, shape, axis)
        return jnp.sum(gauss(at, other, s), axis=axis, keepdims=True)

    sum_y = line(512, spread_ref[2], lax.broadcasted_iota(jnp.int32, (1, 512), 1), 0)
    planes = sp * 2 + lax.broadcasted_iota(jnp.int32, (8, 1), 0)
    sum_z = line(64, spread_ref[0], planes, 1)

    for p in range(2):
        def first(m, carry):
            at = pl.multiple_of(m * 128, 128)
            rows = pl.ds(pl.multiple_of(p * 512 + m * 128, 128), 128)
            sum_x = line(512, spread_ref[1], lax.broadcasted_iota(jnp.int32, (128, 1), 0) + at, 1)
            ones = (sum_x * sum_z[p : p + 1, :]) * sum_y
            hi, lo = split(dens_ref[rows, :] / ones)
            whi[rows, :] = hi
            wlo[rows, :] = lo
            return carry
        lax.fori_loop(0, 4, first, 0)

    pl.semaphore_wait(barrier, len(peers))

    sent = []
    count = [0]

    def remote(src, dst, to):
        n = count[0]
        count[0] += 1
        copy = pltpu.make_async_remote_copy(
            src, dst, send_sem.at[n], recv_sem.at[n], device_id=to, device_id_type=MESH
        )
        copy.start()
        sent.append(copy)
        return copy.wait_recv

    def local(src, dst):
        n = count[0]
        count[0] += 1
        copy = pltpu.make_async_copy(src, dst, recv_sem.at[n])
        copy.start()
        return copy.wait

    pending = {}

    def finish(*key):
        for wait in pending.pop(key):
            wait()

    def slot(ref, lead, axis, k):
        tail = {"y": (slice(None), k), "z": (slice(None), slice(None), k), "x": (slice(None), slice(None), slice(None), k)}
        return ref.at[lead + tail[axis]]

    def swap(src, s_lead, dst, d_lead, axis):
        waits = []
        own = me[axis]
        for k in range(1, SIZE[axis]):
            to = around(axis, k)
            waits.append(remote(slot(src, s_lead, axis, to), slot(dst, d_lead, axis, own), device(**{axis: to})))
        waits.append(local(slot(src, s_lead, axis, own), slot(dst, d_lead, axis, own)))
        return waits

    bufs = (b0, b1, b2)

    def start(a, j, c):
        pending["a2a", a, j, c] = swap(bufs[a], (j, c), bufs[a], (j + 1, c), AXES[a][j])

    wts[0] = jnp.full((8, 128), wt_ref[0], F32)
    pending["wc",] = [remote(wts.at[0], wts.at[1], device(k=1 - core))]

    def weights():
        finish("wc")
        wts[2] = wts[0] + wts[1]
        pending["wh",] = [
            remote(wts.at[2], wts.at[2 + k], device(h=lax.rem(zh + k, 4))) for k in range(1, 4)
        ]

    def total_weight():
        finish("wh")
        wts[6] = 1.0 / (wts[2] + wts[3] + (wts[4] + wts[5]))

    def step_adv(a, j, c):
        finish("a2a", a, j, c)
        start(a, j + 1, c)

    def step_conv(a, h):
        cols = slice(h * 256, h * 256 + 256)

        def along_y(m, carry):
            rows = pl.ds(pl.multiple_of(m * 256, 256), 256)
            x = dot(whi[rows, :], gyh[:, cols]) + (dot(wlo[rows, :], gyh[:, cols]) + dot(whi[rows, :], gyl[:, cols]))
            hi, lo = split(x)
            thi[rows, :] = hi
            tlo[rows, :] = lo
            return carry
        lax.fori_loop(0, 4, along_y, 0)

        for p in range(2):
            def along_x(m, carry):
                rows = pl.ds(pl.multiple_of(m * 128, 128), 128)
                k = slice(p * 512, p * 512 + 512)
                x = dot(gxh[rows, :], thi[k, :]) + (dot(gxl[rows, :], thi[k, :]) + dot(gxh[rows, :], tlo[k, :]))
                for e in range(2):
                    bufs[a][0, 2 * h + e, p, m] = x[:, e * 128 : e * 128 + 128].reshape(2, 4, 16, 128)
                return carry
            lax.fori_loop(0, 4, along_x, 0)
        for e in range(2):
            start(a, 0, 2 * h + e)
        if a == 0 and h == 1:
            weights()

    def columns(x):
        hi, lo = split(x)
        return dot(gz3[...], jnp.concatenate([hi, lo, hi], axis=0))

    own_rows = pl.ds(core * 8, 8)
    other_rows = pl.ds((1 - core) * 8, 8)

    def step_zf(a, c):
        finish("a2a", a, 2, c)
        flat = bufs[a].at[3, c].reshape(1024, 128)
        ph = a // 2
        weight = wt_ref[0]

        def pair(n, carry):
            r = n * 2
            x = jnp.concatenate([flat[pl.ds(r + e, 64, stride=16), :] for e in range(2)], axis=1)
            y = columns(x)
            for e in range(2):
                part = y[:, e * 128 : e * 128 + 128]
                if a == 0:
                    d_ref[c, r + e] = part
                else:
                    part = d_ref[c, r + e] * part
                t_ref[ph, c, r + e] = weight * jnp.log(part)
            return carry
        lax.fori_loop(0, 8, pair, 0)
        pending["cs", ph, c] = [remote(t_ref.at[ph, c, other_rows], cb_ref.at[ph, c], device(k=1 - core))]

    def rows_of(h, n=2, off=0):
        return pl.ds(h * 2 + off, n)

    def step_cs(a, c):
        ph = a // 2
        finish("cs", ph, c)
        u_ref[ph, c] = t_ref[ph, c, own_rows] + cb_ref[ph, c]
        pending["rs1", ph, c] = [
            remote(u_ref.at[ph, c, rows_of(far, 1, 0)], r1_ref.at[ph, c, 0], device(h=right)),
            remote(u_ref.at[ph, c, rows_of(far, 1, 1)], r1_ref.at[ph, c, 1], device(h=left)),
        ]

    def step_rs1(a, c):
        ph = a // 2
        finish("rs1", ph, c)
        u_ref[ph, c, rows_of(right, 1, 0)] += r1_ref[ph, c, 0]
        u_ref[ph, c, rows_of(left, 1, 1)] += r1_ref[ph, c, 1]
        pending["rs2", ph, c] = [
            remote(u_ref.at[ph, c, rows_of(right)], r2_ref.at[ph, c, 0], device(h=right)),
            remote(u_ref.at[ph, c, rows_of(left)], r2_ref.at[ph, c, 1], device(h=left)),
        ]

    def step_rs2(a, c):
        ph = a // 2
        if a == 0 and c == 0:
            total_weight()
        finish("rs2", ph, c)
        total = u_ref[ph, c, rows_of(zh)] + (r2_ref[ph, c, 0] + r2_ref[ph, c, 1])
        mean = jnp.exp(total * wts[6, 0:1, 0:1].reshape(1, 1, 1))
        if a == 0:
            bar_ref[c, rows_of(zh)] = mean
            here = bar_ref.at[c, rows_of(zh)]
            pending["ag1", c] = [remote(here, here, device(h=right)), remote(here, here, device(h=left))]
        else:
            flat = share_ref.at[0].reshape(512, 128)
            for e in range(2):
                flat[pl.ds(c * 2 + e, 64, stride=8), :] = mean[e]

    def step_ag1(a, c):
        finish("ag1", c)
        one = bar_ref.at[c, rows_of(left, 1, 0)]
        two = bar_ref.at[c, rows_of(right, 1, 1)]
        pending["ag2", c] = [remote(one, one, device(h=right)), remote(two, two, device(h=left))]

    def step_ag2(a, c):
        finish("ag2", c)
        pending["cg", c] = [remote(bar_ref.at[c], oth_ref.at[c], device(k=1 - core))]

    def step_zb(a, c):
        flat = b1.at[0, c].reshape(1024, 128)

        def half(src, first):
            def pair(n, carry):
                r = first + n * 2
                parts = []
                for e in range(2):
                    v = src[c, n * 2 + e] / d_ref[c, r + e]
                    d_ref[c, r + e] = v
                    parts.append(v)
                y = columns(jnp.concatenate(parts, axis=1))
                for e in range(2):
                    flat[pl.ds(r + e, 64, stride=16), :] = y[:, e * 128 : e * 128 + 128]
                return carry
            lax.fori_loop(0, 4, pair, 0)

        half(bar_ref, core * 8)
        finish("cg", c)
        half(oth_ref, (1 - core) * 8)
        start(1, 0, c)

    def step_xb(h):
        for e in range(2):
            finish("a2a", 1, 2, 2 * h + e)
        cols = slice(h * 256, h * 256 + 256)
        for p in range(2):
            x = jnp.concatenate([b1[3, 2 * h + e, p].reshape(512, 128) for e in range(2)], axis=1)
            hi, lo = split(x)
            thi[p * 512 : p * 512 + 512, :] = hi
            tlo[p * 512 : p * 512 + 512, :] = lo

            def along_x(m, carry):
                rows = pl.ds(pl.multiple_of(m * 128, 128), 128)
                to = pl.ds(pl.multiple_of(p * 512 + m * 128, 128), 128)
                k = slice(p * 512, p * 512 + 512)
                x = dot(gxh[rows, :], thi[k, :]) + (dot(gxl[rows, :], thi[k, :]) + dot(gxh[rows, :], tlo[k, :]))
                hi, lo = split(x)
                whi[to, cols] = hi
                wlo[to, cols] = lo
                return carry
            lax.fori_loop(0, 4, along_x, 0)

    def step_yb():
        def along_y(m, carry):
            rows = pl.ds(pl.multiple_of(m * 128, 128), 128)
            a_hi, a_lo = whi[rows, :], wlo[rows, :]
            x = dot(a_hi, gyh[...]) + (dot(a_lo, gyh[...]) + dot(a_hi, gyl[...]))
            w = dens_ref[rows, :] / x
            w_ref[rows, :] = w
            hi, lo = split(w)
            whi[rows, :] = hi
            wlo[rows, :] = lo
            return carry
        lax.fori_loop(0, 8, along_y, 0)

    def step_tail():
        for wait in swap(share_ref, (0,), share_ref, (1,), "x"):
            wait()
        for wait in swap(share_ref, (1,), share_ref, (2,), "y"):
            wait()
        for wait in swap(share_ref, (2,), gath_ref, (core, zh), "z"):
            wait()

        def across(*at):
            here = gath_ref.at[(core,) + at]
            return remote(here, here, device(k=1 - core))

        here = gath_ref.at[core, zh]
        ring = [remote(here, here, device(h=right)), remote(here, here, device(h=left))]
        over = [across(zh)]
        for wait in ring:
            wait()
        one, two = gath_ref.at[core, left, 0], gath_ref.at[core, right, 1]
        ring = [remote(one, one, device(h=right)), remote(two, two, device(h=left))]
        over += [across(left), across(right)]
        for wait in ring:
            wait()
        over += [across(far)]
        for wait in over:
            wait()

        def place(n, carry):
            src = gath_ref.at[n >> 2, n & 3].reshape(512, 128)
            for c in range(CH):
                for e in range(2):
                    dst = bary_ref.at[c]
                    dst[pl.ds(n * 2 + e, 64, stride=16), :] = src[pl.ds(c * 2 + e, 64, stride=8), :]
            return carry
        lax.fori_loop(0, 8, place, 0)

    table = {
        "conv": step_conv, "adv": step_adv, "zf": step_zf, "cs": step_cs, "rs1": step_rs1, "rs2": step_rs2,
        "ag1": step_ag1, "ag2": step_ag2, "zb": step_zb, "xb": step_xb, "yb": step_yb, "tail": step_tail,
    }
    for name, *rest in order():
        table[name](*rest)
    for copy in sent:
        copy.wait_send()
    assert count[0] <= SEMS and not pending


SEMS = 240


def local(densities, weights, spreads):
    field = (4, CH, 2, 4, 2, 4, 16, 128)
    vmem = pltpu.VMEM
    scratch = [
        vmem(field, F32), vmem(field, F32), vmem(field, F32),
        vmem((CH, 16, 64, 128), F32),
        vmem((2, CH, 16, 64, 128), F32),
        vmem((2, CH, 8, 64, 128), F32),
        vmem((2, CH, 8, 64, 128), F32),
        vmem((2, CH, 2, 1, 64, 128), F32),
        vmem((2, CH, 2, 2, 64, 128), F32),
        vmem((CH, 8, 64, 128), F32),
        vmem((CH, 8, 64, 128), F32),
        vmem((3, 2, 4, 2, 4, 8, 128), F32),
        vmem((2, 4, 2, 4, 2, 4, 8, 128), F32),
        vmem((1024, 512), BF), vmem((1024, 512), BF),
        vmem((1024, 256), BF), vmem((1024, 256), BF),
        vmem((512, 512), BF), vmem((512, 512), BF), vmem((512, 512), BF), vmem((512, 512), BF),
        vmem((64, 192), BF),
        vmem((7, 8, 128), F32),
        pltpu.SemaphoreType.DMA((SEMS,)), pltpu.SemaphoreType.DMA((SEMS,)),
    ]
    whole = pl.BlockSpec(memory_space=pltpu.VMEM)
    smem = pl.BlockSpec(memory_space=pltpu.SMEM)
    bary, scale_w = pl.pallas_call(
        body,
        out_shape=[
            jax.ShapeDtypeStruct((CH, 1024, 128), F32),
            jax.ShapeDtypeStruct((1024, 512), F32),
        ],
        in_specs=[whole, smem, smem],
        out_specs=[whole, whole],
        scratch_shapes=scratch,
        compiler_params=pltpu.CompilerParams(
            collective_id=0, has_side_effects=True, vmem_limit_bytes=61 * 1024 * 1024
        ),
        name="sinkhorn",
    )(densities.reshape(1024, 512), weights, spreads)
    bary = bary.reshape(CH, 2, 512, 128).transpose(1, 2, 0, 3).reshape(2, 512, 512)
    return bary, scale_w.reshape(1, 2, 512, 512)


def solution(mesh):
    return jax.shard_map(
        local,
        mesh=mesh,
        in_specs=(P("dens", "sp", None, None), P("dens"), P()),
        out_specs=(P("sp", None, None), P("dens", "sp", None, None)),
        check_vma=False,
    )
```

time: 568 us -> 234 us (0.41); the launches traced: 560 us -> 233 us
  Pallas kernels: 0 us -> 227 us
  blocking collectives: 218 us -> 0 us
  waiting for transfers between devices: 197 us -> 0 us
  matrix products: 50 us -> 0 us
  local copies, waits for them, and re-layouts: 46.1 us -> 4.67 us
  starting transfers between devices: 16.5 us -> 0 us
  between operations: 17.3 us -> 1.29 us
  other arithmetic: 14.9 us -> 0 us
    pallas_call x0 -> x1, Pallas kernels: none -> 227 us  [local(): pl.pallas_call(body, out_shape=[jax.ShapeDtypeStruct((CH, 1024, 128), F32...]
    all_to_all x6 -> x0, blocking collectives: 198 us -> none  [the longest x3 99.6 us: to_columns(): return lax.all_to_all(field, 'sp', split_axis=1, concat_axis=0, tiled=True)]
    psum x2 -> x0, waiting for transfers between devices: 145 us -> none  [local(): summed = lax.psum(term, 'dens')]
    all_to_all x2 -> x0, waiting for transfers between devices: 52.4 us -> none  [the longest x1 26.5 us: to_columns(): return lax.all_to_all(field, 'sp', split_axis=1, concat_axis=0, tiled=True)]
    dot_general x12 -> x0, matrix products: 50 us -> none  [the longest x4 17.7 us: along_planes(): field = jnp.einsum('zxy,yk->zxk', field, kern_y, precision=hp)]
    all_to_all x12 -> x0, local copies, waits for them, and re-layouts: 25.7 us -> none  [the longest x8 23.4 us: to_columns(): return lax.all_to_all(field, 'sp', split_axis=1, concat_axis=0, tiled=True)]
    psum x1 -> x0, blocking collectives: 19.9 us -> none  [local(): total_weight = lax.psum(weights[0], 'dens')]
    all_to_all x2 -> x0, starting transfers between devices: 16.5 us -> none  [the longest x1 9.44 us: to_columns(): return lax.all_to_all(field, 'sp', split_axis=1, concat_axis=0, tiled=True)]
  transfers between devices with their start and end apart: 4 -> 0, of which waited for: 4 -> 0; matrix products, arithmetic and copies ran while one was open for 1% -> 0% of each run, Pallas kernels for 0% -> 0%
where the time goes in v1:
time: 234 us; the launch traced here: 233 us
  Pallas kernels  227 us (97%)
  local copies, waits for them, and re-layouts  4.67 us (2%)
    pallas_call x1, Pallas kernels, local(): pl.pallas_call(body, out_shape=[jax.ShapeDtypeStruct((CH, 1024, 128), F32...  227 us

profile of v1, /device:TPU:1, one launch (start us, length us, event | category | flops | bytes accessed | tf_op | source)
XLA Modules:
  0.0 233.0 jit_solution(15191165727583102432)
XLA Ops:
  1.3 227.0 %sinkhorn.1 = (f32[4,1024,128]{2,1,0:T(8,128)}, f32[1024,512]{1,0:T(8,128)}) custom-call(f32[1024,512]{1,0:T(8,128)} %bitcast.9, f32[1]{0:T(128)S(6)} %copy.10.wt_ref, f32[3]{0:T(128)} %spread_ref.1), custom_call_target="tpu_custom_call" | custom-call | tf_op jit(solution)/shard_map/sinkhorn/pallas_call | solution.py:423
  228.3 0.0 copy-start
  228.3 3.4 %copy.8 = f32[4,2,64,8,128]{4,3,0,2,1:T(8,128)} copy(f32[4,2,64,8,128]{4,3,2,1,0:T(8,128)} %bitcast.12) | data formatting | bytes 4194304 | tf_op jit(solution)/shard_map/reshape | solution.py:437
  231.6 0.0 copy-done
  231.7 1.3 copy.11
Async XLA Ops:
  228.3 3.4 %copy-start = (f32[1024,512]{1,0:T(8,128)S(1)}, f32[1024,512]{1,0:T(8,128)}, u32[]{:S(2)}) copy-start(f32[1024,512]{1,0:T(8,128)} %get-tuple-element.5) | copy-start | bytes 6291460

commit v2 on v1

--- a/solution.py
+++ b/solution.py
@@ -15,30 +15,26 @@
 NXD, NYD, NZD, NHD = 4, 4, 2, 4
 CH = 4
 SIZE = {"x": NXD, "y": NYD, "z": NZD}
-AXES = (("z", "x", "y"), ("z", "x", "y"), ("z", "x", "y"))
-
-
-def order():
-    steps = []
-    steps += [("conv", 0, 0), ("conv", 0, 1)]
-    flow = [("adv", 0, 0), ("adv", 0, 1), ("zf", 0), ("cs", 0), ("rs1", 0), ("rs2", 0), ("ag1", 0), ("ag2", 0), ("zb", 0), ("adv", 1, 0), ("adv", 1, 1)]
-    when = [6.5, 13, 20, 22.5, 26, 30.5, 35, 38.5, 41, 47, 53.5]
-    lag = [5, 5, 4, 4, 4.5, 5, 5.5, 5.5, 5.5, 5.5, 5.5]
-    timed = []
-    for c in range(CH):
-        for i, step in enumerate(flow):
-            timed.append((when[i] + c * lag[i], i, step + (c,)))
-    steps += [t[2] for t in sorted(timed)]
-    steps += [("xb", 0), ("xb", 1), ("yb",)]
-    steps += [("conv", 2, 0), ("conv", 2, 1)]
-    flow = [("adv", 2, 0), ("adv", 2, 1), ("zf", 2), ("cs", 2), ("rs1", 2), ("rs2", 2)]
-    timed = []
-    for c in range(CH):
-        for i, step in enumerate(flow):
-            timed.append((when[i] + c * lag[i], i, step + (c,)))
-    steps += [t[2] for t in sorted(timed)]
-    steps += [("tail",)]
-    return steps
+AXES = (
+    ("zxy", "xyz", "zxy", "zyx"),
+    ("xyz", "xyz", "xyz", "zxy"),
+    ("xyz", "zxy", "yxz", "zxy"),
+)
+
+
+ORDER = (
+    ("conv", 0, 0), ("conv", 0, 1), ("adv", 0, 0, 0), ("adv", 0, 0, 1), ("adv", 0, 0, 2), ("adv", 0, 1, 0), ("adv", 0, 1, 1),
+    ("adv", 0, 0, 3), ("adv", 0, 1, 2), ("zf", 0, 0), ("zf", 0, 1), ("cs", 0, 0), ("cs", 0, 1), ("adv", 0, 1, 3), ("rs1", 0, 0),
+    ("rs1", 0, 1), ("zf", 0, 2), ("rs2", 0, 0), ("zf", 0, 3), ("cs", 0, 2), ("rs2", 0, 1), ("cs", 0, 3), ("ag1", 0, 0),
+    ("rs1", 0, 2), ("ag1", 0, 1), ("rs1", 0, 3), ("ag2", 0, 0), ("rs2", 0, 2), ("zb", 0, 0), ("ag2", 0, 1), ("rs2", 0, 3),
+    ("zb", 0, 1), ("ag1", 0, 2), ("ag1", 0, 3), ("adv", 1, 0, 0), ("ag2", 0, 2), ("ag2", 0, 3), ("zb", 0, 2), ("adv", 1, 0, 1),
+    ("zb", 0, 3), ("adv", 1, 1, 0), ("adv", 1, 0, 2), ("adv", 1, 1, 1), ("adv", 1, 0, 3), ("adv", 1, 1, 2), ("adv", 1, 1, 3),
+    ("xb", 0), ("xb", 1), ("yb",), ("conv", 2, 0), ("conv", 2, 1), ("adv", 2, 0, 0), ("adv", 2, 0, 1), ("adv", 2, 0, 2),
+    ("adv", 2, 0, 3), ("adv", 2, 1, 0), ("adv", 2, 1, 1), ("adv", 2, 1, 2), ("zf", 2, 0), ("zf", 2, 1), ("adv", 2, 1, 3),
+    ("cs", 2, 0), ("cs", 2, 1), ("zf", 2, 2), ("rs1", 2, 0), ("rs1", 2, 1), ("cs", 2, 2), ("zf", 2, 3), ("rs2", 2, 0),
+    ("cs", 2, 3), ("rs2", 2, 1), ("tx", 0), ("rs1", 2, 2), ("rs1", 2, 3), ("ty", 0), ("rs2", 2, 2), ("tz", 0), ("rs2", 2, 3),
+    ("tx", 1), ("tg", 0), ("ty", 1), ("tz", 1), ("th", 0), ("tg", 1), ("ti", 0), ("tp", 0), ("th", 1), ("ti", 1), ("tp", 1),
+)
 
 
 def split(x):
@@ -51,9 +47,9 @@
 
 
 def body(
-    dens_ref, wt_ref, spread_ref, bary_ref, w_ref,
-    b0, b1, b2, d_ref, t_ref, cb_ref, u_ref, r1_ref, r2_ref, bar_ref, oth_ref,
-    share_ref, gath_ref, whi, wlo, thi, tlo, gxh, gxl, gyh, gyl, gz3, wts, send_sem, recv_sem,
+    dens_hbm, wt_ref, spread_ref, bary_hbm, w_hbm,
+    dens_ref, w_ref, bary_ref, inv_x, b0, b1, b2, d_ref, t_ref, cb_ref, u_ref, r1_ref, r2_ref, bar_ref, oth_ref,
+    share_ref, gath_ref, whi, wlo, thi, tlo, gxh, gxl, gyh, gyl, gz3, wts, io_sem, send_sem, recv_sem,
 ):
     dens = lax.axis_index("dens")
     sp = lax.axis_index("sp")
@@ -76,25 +72,31 @@
     for peer in peers:
         pl.semaphore_signal(barrier, 1, device_id=peer, device_id_type=MESH)
 
+    fetch = pltpu.make_async_copy(dens_hbm, dens_ref, io_sem.at[0])
+    fetch.start()
     root = math.sqrt(math.pi)
 
     def gauss(i, j, s):
-        diff = (i.astype(F32) - j.astype(F32)) / s
-        return jnp.exp(-diff * diff) / (s * jnp.float32(root))
+        diff = (i - j).astype(F32) * (1.0 / s)
+        return jnp.exp(-diff * diff) * (1.0 / (s * jnp.float32(root)))
 
     def wide(hi_ref, lo_ref, s):
-        def tile(m, carry):
-            at = pl.multiple_of(m * 128, 128)
-            i = lax.broadcasted_iota(jnp.int32, (128, 512), 0) + at
-            j = lax.broadcasted_iota(jnp.int32, (128, 512), 1)
-            hi, lo = split(gauss(i, j, s))
-            hi_ref[pl.ds(at, 128), :] = hi
-            lo_ref[pl.ds(at, 128), :] = lo
-            return carry
-        lax.fori_loop(0, 4, tile, 0)
-
+        def tile(m, total):
+            at = pl.multiple_of(m * 64, 64)
+            i = lax.broadcasted_iota(jnp.int32, (64, 512), 0) + at
+            j = lax.broadcasted_iota(jnp.int32, (64, 512), 1)
+            g = gauss(i, j, s)
+            hi, lo = split(g)
+            hi_ref[pl.ds(at, 64), :] = hi
+            lo_ref[pl.ds(at, 64), :] = lo
+            if hi_ref is gxh:
+                inv_x[pl.ds(at, 64), :] = jnp.broadcast_to(1.0 / jnp.sum(g, axis=1, keepdims=True), (64, 128))
+                return total
+            return total + jnp.sum(g, axis=0, keepdims=True)
+        return lax.fori_loop(0, 8, tile, jnp.zeros((1, 512), F32))
+
+    sum_y = wide(gyh, gyl, spread_ref[2])
     wide(gxh, gxl, spread_ref[1])
-    wide(gyh, gyl, spread_ref[2])
 
     def plane(q):
         return ((q >> 3) & 3) * 16 + ((q >> 2) & 1) * 8 + (q & 3) * 2 + (q >> 5)
@@ -104,30 +106,28 @@
     hi, lo = split(gauss(plane(i), plane(j & 63), spread_ref[0]))
     gz3[...] = jnp.where(j < 128, hi.astype(F32), lo.astype(F32)).astype(BF)
 
-    def line(n, s, at, axis):
-        shape = (at.shape[0], n) if axis == 1 else (n, at.shape[1])
-        other = lax.broadcasted_iota(jnp.int32, shape, axis)
-        return jnp.sum(gauss(at, other, s), axis=axis, keepdims=True)
-
-    sum_y = line(512, spread_ref[2], lax.broadcasted_iota(jnp.int32, (1, 512), 1), 0)
-    planes = sp * 2 + lax.broadcasted_iota(jnp.int32, (8, 1), 0)
-    sum_z = line(64, spread_ref[0], planes, 1)
-
+    planes = sp * 2 + lax.broadcasted_iota(jnp.int32, (8, 128), 0)
+    others = lax.broadcasted_iota(jnp.int32, (8, 128), 1)
+    near = jnp.where(others < 64, gauss(planes, others, spread_ref[0]), 0.0)
+    sum_z = jnp.sum(near, axis=1, keepdims=True)
+
+    fetch.wait()
     for p in range(2):
+        inv_y = 1.0 / (sum_y * sum_z[p : p + 1, :])
+
         def first(m, carry):
-            at = pl.multiple_of(m * 128, 128)
-            rows = pl.ds(pl.multiple_of(p * 512 + m * 128, 128), 128)
-            sum_x = line(512, spread_ref[1], lax.broadcasted_iota(jnp.int32, (128, 1), 0) + at, 1)
-            ones = (sum_x * sum_z[p : p + 1, :]) * sum_y
-            hi, lo = split(dens_ref[rows, :] / ones)
+            rows = pl.ds(pl.multiple_of(p * 512 + m * 64, 64), 64)
+            inv = inv_x[pl.ds(pl.multiple_of(m * 64, 64), 64), :]
+            hi, lo = split(dens_ref[rows, :] * jnp.concatenate([inv] * 4, axis=1) * inv_y)
             whi[rows, :] = hi
             wlo[rows, :] = lo
             return carry
-        lax.fori_loop(0, 4, first, 0)
+        lax.fori_loop(0, 8, first, 0)
 
     pl.semaphore_wait(barrier, len(peers))
 
     sent = []
+    outs = []
     count = [0]
 
     def remote(src, dst, to):
@@ -157,19 +157,24 @@
         tail = {"y": (slice(None), k), "z": (slice(None), slice(None), k), "x": (slice(None), slice(None), slice(None), k)}
         return ref.at[lead + tail[axis]]
 
-    def swap(src, s_lead, dst, d_lead, axis):
+    def swap(src, s_lead, dst, d_lead, axis, h=None):
         waits = []
         own = me[axis]
+
+        def piece(ref, lead, k):
+            ref = slot(ref, lead, axis, k)
+            return ref if h is None else part(ref, h)
+
         for k in range(1, SIZE[axis]):
             to = around(axis, k)
-            waits.append(remote(slot(src, s_lead, axis, to), slot(dst, d_lead, axis, own), device(**{axis: to})))
-        waits.append(local(slot(src, s_lead, axis, own), slot(dst, d_lead, axis, own)))
+            waits.append(remote(piece(src, s_lead, to), piece(dst, d_lead, own), device(**{axis: to})))
+        waits.append(local(piece(src, s_lead, own), piece(dst, d_lead, own)))
         return waits
 
     bufs = (b0, b1, b2)
 
     def start(a, j, c):
-        pending["a2a", a, j, c] = swap(bufs[a], (j, c), bufs[a], (j + 1, c), AXES[a][j])
+        pending["a2a", a, j, c] = swap(bufs[a], (j, c), bufs[a], (j + 1, c), AXES[a][c][j])
 
     wts[0] = jnp.full((8, 128), wt_ref[0], F32)
     pending["wc",] = [remote(wts.at[0], wts.at[1], device(k=1 - core))]
@@ -228,20 +233,24 @@
         ph = a // 2
         weight = wt_ref[0]
 
-        def pair(n, carry):
-            r = n * 2
-            x = jnp.concatenate([flat[pl.ds(r + e, 64, stride=16), :] for e in range(2)], axis=1)
-            y = columns(x)
-            for e in range(2):
-                part = y[:, e * 128 : e * 128 + 128]
-                if a == 0:
-                    d_ref[c, r + e] = part
-                else:
-                    part = d_ref[c, r + e] * part
-                t_ref[ph, c, r + e] = weight * jnp.log(part)
-            return carry
-        lax.fori_loop(0, 8, pair, 0)
+        def half(first):
+            def pair(n, carry):
+                r = first + n * 2
+                x = jnp.concatenate([flat[pl.ds(r + e, 64, stride=16), :] for e in range(2)], axis=1)
+                y = columns(x)
+                for e in range(2):
+                    part = y[:, e * 128 : e * 128 + 128]
+                    if a == 0:
+                        d_ref[c, r + e] = part
+                    else:
+                        part = d_ref[c, r + e] * part
+                    t_ref[ph, c, r + e] = weight * jnp.log(part)
+                return carry
+            lax.fori_loop(0, 4, pair, 0)
+
+        half((1 - core) * 8)
         pending["cs", ph, c] = [remote(t_ref.at[ph, c, other_rows], cb_ref.at[ph, c], device(k=1 - core))]
+        half(core * 8)
 
     def rows_of(h, n=2, off=0):
         return pl.ds(h * 2 + off, n)
@@ -346,60 +355,92 @@
             wlo[rows, :] = lo
             return carry
         lax.fori_loop(0, 8, along_y, 0)
-
-    def step_tail():
-        for wait in swap(share_ref, (0,), share_ref, (1,), "x"):
-            wait()
-        for wait in swap(share_ref, (1,), share_ref, (2,), "y"):
-            wait()
-        for wait in swap(share_ref, (2,), gath_ref, (core, zh), "z"):
-            wait()
-
-        def across(*at):
-            here = gath_ref.at[(core,) + at]
-            return remote(here, here, device(k=1 - core))
-
-        here = gath_ref.at[core, zh]
-        ring = [remote(here, here, device(h=right)), remote(here, here, device(h=left))]
-        over = [across(zh)]
-        for wait in ring:
-            wait()
-        one, two = gath_ref.at[core, left, 0], gath_ref.at[core, right, 1]
-        ring = [remote(one, one, device(h=right)), remote(two, two, device(h=left))]
-        over += [across(left), across(right)]
-        for wait in ring:
-            wait()
-        over += [across(far)]
-        for wait in over:
-            wait()
-
-        def place(n, carry):
-            src = gath_ref.at[n >> 2, n & 3].reshape(512, 128)
-            for c in range(CH):
-                for e in range(2):
-                    dst = bary_ref.at[c]
-                    dst[pl.ds(n * 2 + e, 64, stride=16), :] = src[pl.ds(c * 2 + e, 64, stride=8), :]
-            return carry
-        lax.fori_loop(0, 8, place, 0)
+        copy = pltpu.make_async_copy(w_ref, w_hbm, io_sem.at[1])
+        copy.start()
+        outs.append(copy)
+
+    def part(ref, h):
+        return ref.at[..., pl.ds(h * 4, 4), :]
+
+    def step_tx(h):
+        pending["tail", h] = swap(share_ref, (0,), share_ref, (1,), "x", h)
+
+    def step_ty(h):
+        finish("tail", h)
+        pending["tail", h] = swap(share_ref, (1,), share_ref, (2,), "y", h)
+
+    def step_tz(h):
+        finish("tail", h)
+        pending["tail", h] = swap(share_ref, (2,), gath_ref, (core, zh), "z", h)
+
+    def both(one, two):
+        return [remote(one, one, device(h=right)), remote(two, two, device(h=left))]
+
+    def across(h, *at):
+        here = part(gath_ref.at[(core,) + at], h)
+        pending["over", h].append(remote(here, here, device(k=1 - core)))
+
+    def step_tg(h):
+        finish("tail", h)
+        here = part(gath_ref.at[core, zh], h)
+        pending["tail", h] = both(here, here)
+        pending["over", h] = []
+        across(h, zh)
+
+    def step_th(h):
+        finish("tail", h)
+        pending["tail", h] = both(part(gath_ref.at[core, left, 0], h), part(gath_ref.at[core, right, 1], h))
+        across(h, left)
+        across(h, right)
+
+    def step_ti(h):
+        finish("tail", h)
+        across(h, far)
+
+    def step_tp(h):
+        def place(k):
+            def block(zz, carry):
+                n = k * 4 + zz
+                src = gath_ref.at[k, zz].reshape(512, 128)
+                for c in (2 * h, 2 * h + 1):
+                    for e in range(2):
+                        dst = bary_ref.at[c]
+                        dst[pl.ds(n * 2 + e, 64, stride=16), :] = src[pl.ds(c * 2 + e, 64, stride=8), :]
+                return carry
+            lax.fori_loop(0, 4, block, 0)
+
+        place(core)
+        finish("over", h)
+        place(1 - core)
+        for c in (2 * h, 2 * h + 1):
+            copy = pltpu.make_async_copy(bary_ref.at[c], bary_hbm.at[:, pl.ds(c * 128, 128)], io_sem.at[2 + c])
+            copy.start()
+            outs.append(copy)
 
     table = {
         "conv": step_conv, "adv": step_adv, "zf": step_zf, "cs": step_cs, "rs1": step_rs1, "rs2": step_rs2,
-        "ag1": step_ag1, "ag2": step_ag2, "zb": step_zb, "xb": step_xb, "yb": step_yb, "tail": step_tail,
+        "ag1": step_ag1, "ag2": step_ag2, "zb": step_zb, "xb": step_xb, "yb": step_yb,
+        "tx": step_tx, "ty": step_ty, "tz": step_tz, "tg": step_tg, "th": step_th, "ti": step_ti, "tp": step_tp,
     }
-    for name, *rest in order():
+    for name, *rest in ORDER:
+        while len(sent) > 40:
+            sent.pop(0).wait_send()
         table[name](*rest)
     for copy in sent:
         copy.wait_send()
+    for copy in outs:
+        copy.wait()
     assert count[0] <= SEMS and not pending
 
 
-SEMS = 240
+SEMS = 260
 
 
 def local(densities, weights, spreads):
     field = (4, CH, 2, 4, 2, 4, 16, 128)
     vmem = pltpu.VMEM
     scratch = [
+        vmem((1024, 512), F32), vmem((1024, 512), F32), vmem((CH, 1024, 128), F32), vmem((512, 128), F32),
         vmem(field, F32), vmem(field, F32), vmem(field, F32),
         vmem((CH, 16, 64, 128), F32),
         vmem((2, CH, 16, 64, 128), F32),
@@ -416,14 +457,14 @@
         vmem((512, 512), BF), vmem((512, 512), BF), vmem((512, 512), BF), vmem((512, 512), BF),
         vmem((64, 192), BF),
         vmem((7, 8, 128), F32),
-        pltpu.SemaphoreType.DMA((SEMS,)), pltpu.SemaphoreType.DMA((SEMS,)),
+        pltpu.SemaphoreType.DMA((6,)), pltpu.SemaphoreType.DMA((SEMS,)), pltpu.SemaphoreType.DMA((SEMS,)),
     ]
-    whole = pl.BlockSpec(memory_space=pltpu.VMEM)
+    whole = pl.BlockSpec(memory_space=pl.ANY)
     smem = pl.BlockSpec(memory_space=pltpu.SMEM)
     bary, scale_w = pl.pallas_call(
         body,
         out_shape=[
-            jax.ShapeDtypeStruct((CH, 1024, 128), F32),
+            jax.ShapeDtypeStruct((1024, 512), F32),
             jax.ShapeDtypeStruct((1024, 512), F32),
         ],
         in_specs=[whole, smem, smem],
@@ -434,8 +475,7 @@
         ),
         name="sinkhorn",
     )(densities.reshape(1024, 512), weights, spreads)
-    bary = bary.reshape(CH, 2, 512, 128).transpose(1, 2, 0, 3).reshape(2, 512, 512)
-    return bary, scale_w.reshape(1, 2, 512, 512)
+    return bary.reshape(2, 512, 512), scale_w.reshape(1, 2, 512, 512)
 
 
 def solution(mesh):

time: 234 us -> 207 us (0.88)
  Pallas kernels: 227 us -> 201 us
    pallas_call x1, Pallas kernels: 227 us -> 201 us  [local(): pl.pallas_call(body, out_shape=[jax.ShapeDtypeStruct((1024, 512), F32), j...]
    reshape x1 -> x0, local copies, waits for them, and re-layouts: 3.35 us -> none  [local(): bary.reshape(CH, 2, 512, 128).transpose(1, 2, 0, 3).reshape(2, 512, 512)]
    unnamed x3 -> x4, local copies, waits for them, and re-layouts: 1.32 us -> 4.55 us
where the time goes in v2:
time: 207 us
  Pallas kernels  201 us (97%)
  local copies, waits for them, and re-layouts  4.55 us (2%)
    pallas_call x1, Pallas kernels, local(): pl.pallas_call(body, out_shape=[jax.ShapeDtypeStruct((1024, 512), F32), j...  201 us
    unnamed x4, local copies, waits for them, and re-layouts  4.55 us

profile of v2, /device:TPU:1, one launch (start us, length us, event | category | flops | bytes accessed | tf_op | source)
XLA Modules:
  0.0 207.3 jit_solution(16100113792431436315)
XLA Ops:
  1.3 201.4 %sinkhorn.1 = (f32[1024,512]{1,0:T(8,128)}, f32[1024,512]{1,0:T(8,128)}) custom-call(f32[1024,512]{1,0:T(8,128)} %bitcast.3, f32[1]{0:T(128)S(6)} %copy.7.wt_ref, f32[3]{0:T(128)} %spread_ref.1), custom_call_target="tpu_custom_call" | custom-call | tf_op jit(solution)/shard_map/sinkhorn/pallas_call | solution.py:464
  202.7 0.0 copy-start
  202.7 3.2 %copy.8 = f32[2,512,512]{2,1,0:T(8,128)} copy(f32[2,512,512]{2,1,0:T(8,128)} %bitcast.5) | data formatting | bytes 4194304
  206.0 0.0 copy-done
  206.0 1.3 copy.9
Async XLA Ops:
  202.7 3.2 %copy-start = (f32[1024,512]{1,0:T(8,128)S(1)}, f32[1024,512]{1,0:T(8,128)}, u32[]{:S(2)}) copy-start(f32[1024,512]{1,0:T(8,128)} %get-tuple-element.5) | copy-start | bytes 6291460

commit v3 on v2

v3 whole, which is shorter than its diff:
```python
import functools
import math

import jax
import jax.numpy as jnp
from jax import lax
from jax.experimental import pallas as pl
from jax.experimental.pallas import tpu as pltpu
from jax.sharding import PartitionSpec as P

MESH = pl.DeviceIdType.MESH
BF = jnp.bfloat16
F32 = jnp.float32

NXD, NYD, NZD, NHD = 4, 4, 2, 4
CH = 4
SIZE = {"x": NXD, "y": NYD, "z": NZD}
AXES = (
    (("yxz", "yzx"), ("zyx", "xzy"), ("yxz", "zyx"), ("xyz", "yzx")),
    (("zyx", "xyz"), ("yxz", "xyz"), ("xzy", "zyx"), ("xyz", "zxy")),
    (("yzx", "yzx"), ("zxy", "xyz"), ("xzy", "xzy"), ("yzx", "yxz")),
)


ORDER = (
    ("conv", 0, 0), ("conv", 0, 1), ("adv", 0, 0, 0, 0), ("adv", 0, 0, 1, 0), ("adv", 0, 0, 1, 1), ("adv", 0, 0, 0, 1),
    ("adv", 0, 0, 2, 1), ("adv", 0, 0, 3, 0), ("adv", 0, 0, 2, 0), ("adv", 0, 1, 0, 0), ("adv", 0, 1, 1, 1), ("adv", 0, 0, 3, 1),
    ("adv", 0, 1, 0, 1), ("adv", 0, 1, 2, 0), ("adv", 0, 1, 1, 0), ("zo", 0, 0), ("adv", 0, 1, 2, 1), ("zw", 0, 0),
    ("adv", 0, 1, 3, 1), ("cs", 0, 0), ("adv", 0, 1, 3, 0), ("zo", 0, 1), ("zo", 0, 2), ("zw", 0, 1), ("zw", 0, 2), ("cs", 0, 1),
    ("rs1", 0, 0), ("cs", 0, 2), ("zo", 0, 3), ("zw", 0, 3), ("cs", 0, 3), ("rs1", 0, 1), ("rs2", 0, 0), ("rs1", 0, 2),
    ("rs1", 0, 3), ("rs2", 0, 1), ("ag1", 0, 0), ("rs2", 0, 2), ("rs2", 0, 3), ("ag1", 0, 1), ("ag2", 0, 0), ("zbw", 0, 0),
    ("ag1", 0, 2), ("ag1", 0, 3), ("zbo", 0, 0), ("ag2", 0, 1), ("zbw", 0, 1), ("adv", 1, 0, 0, 1), ("ag2", 0, 2), ("zbw", 0, 2),
    ("zbo", 0, 1), ("adv", 1, 0, 0, 0), ("ag2", 0, 3), ("zbw", 0, 3), ("zbo", 0, 2), ("adv", 1, 0, 1, 1), ("adv", 1, 1, 0, 1),
    ("zbo", 0, 3), ("adv", 1, 0, 2, 1), ("adv", 1, 0, 1, 0), ("adv", 1, 0, 3, 1), ("adv", 1, 0, 2, 0), ("adv", 1, 1, 0, 0),
    ("adv", 1, 0, 3, 0), ("adv", 1, 1, 1, 1), ("adv", 1, 1, 2, 0), ("adv", 1, 1, 1, 0), ("adv", 1, 1, 2, 1), ("adv", 1, 1, 3, 0),
    ("adv", 1, 1, 3, 1), ("xb", 0), ("xb", 1), ("yb",), ("conv", 2, 0), ("conv", 2, 1), ("adv", 2, 0, 0, 0), ("adv", 2, 0, 1, 0),
    ("adv", 2, 0, 1, 1), ("adv", 2, 0, 0, 1), ("adv", 2, 0, 2, 0), ("adv", 2, 1, 0, 0), ("adv", 2, 0, 2, 1), ("adv", 2, 0, 3, 0),
    ("adv", 2, 1, 0, 1), ("adv", 2, 0, 3, 1), ("adv", 2, 1, 1, 0), ("adv", 2, 1, 2, 0), ("adv", 2, 1, 1, 1), ("zo", 2, 0),
    ("adv", 2, 1, 2, 1), ("zw", 2, 0), ("zo", 2, 1), ("cs", 2, 0), ("adv", 2, 1, 3, 0), ("adv", 2, 1, 3, 1), ("zo", 2, 2),
    ("zw", 2, 1), ("zw", 2, 2), ("cs", 2, 1), ("cs", 2, 2), ("rs1", 2, 0), ("zo", 2, 3), ("zw", 2, 3), ("cs", 2, 3),
    ("rs1", 2, 1), ("rs1", 2, 2), ("rs2", 2, 0), ("rs1", 2, 3), ("rs2", 2, 1), ("tx", 0), ("rs2", 2, 2), ("rs2", 2, 3), ("tx", 1),
    ("ty", 0), ("ty", 1), ("tz", 0), ("tz", 1), ("tg", 0), ("tg", 1), ("th", 0), ("th", 1), ("ti", 0), ("ti", 1), ("tp", 0),
    ("tp", 1),
)


def split(x):
    hi = x.astype(BF)
    return hi, (x - hi.astype(F32)).astype(BF)


def dot(a, b):
    return jnp.dot(a, b, preferred_element_type=F32)


def body(
    dens_hbm, wt_ref, spread_ref, bary_hbm, w_hbm,
    dens_ref, w_ref, bary_ref, inv_x, b0, b1, b2, d_ref, t_ref, cb_ref, u_ref, r1_ref, r2_ref, bar_ref, oth_ref,
    share_ref, gath_ref, whi, wlo, thi, tlo, gxh, gxl, gyh, gyl, gz3, wts, io_sem, send_sem, recv_sem,
):
    dens = lax.axis_index("dens")
    sp = lax.axis_index("sp")
    zh, core = dens // 2, lax.rem(dens, 2)
    me = {"y": sp // 8, "z": lax.rem(sp // 4, 2), "x": lax.rem(sp, 4)}

    def device(h=zh, k=core, **at):
        at = {**me, **at}
        return {"dens": h * 2 + k, "sp": (at["y"] * 2 + at["z"]) * 4 + at["x"]}

    def around(axis, k):
        return lax.rem(me[axis] + k, SIZE[axis])

    right, left = lax.rem(zh + 1, 4), lax.rem(zh + 3, 4)
    far = lax.rem(zh + 2, 4)
    zl = me["z"]
    eff = lax.rem(zl + zh, 2)
    one = device(h=lax.rem(zh + 3 + 2 * zl, 4), z=1 - zl)
    two = device(h=lax.rem(zh + 1 + 2 * zl, 4), z=1 - zl)
    gray = lax.rem(zh + zh // 2, 2)
    bit_one = (zh // 2) * (1 - eff) + gray * eff
    bit_two = gray * (1 - eff) + (zh // 2) * eff
    quarter = bit_one * 2 + bit_two
    peers = [device(**{axis: around(axis, k)}) for axis in "xyz" for k in range(1, SIZE[axis])]
    peers += [device(k=1 - core), device(h=right), device(h=left), device(h=far), one, two]

    barrier = pltpu.get_barrier_semaphore()
    for peer in peers:
        pl.semaphore_signal(barrier, 1, device_id=peer, device_id_type=MESH)

    fetch = pltpu.make_async_copy(dens_hbm, dens_ref, io_sem.at[0])
    fetch.start()
    root = math.sqrt(math.pi)

    def gauss(i, j, s):
        diff = (i - j).astype(F32) * (1.0 / s)
        return jnp.exp(-diff * diff) * (1.0 / (s * jnp.float32(root)))

    def wide(hi_ref, lo_ref, s):
        def tile(m, total):
            at = pl.multiple_of(m * 64, 64)
            i = lax.broadcasted_iota(jnp.int32, (64, 512), 0) + at
            j = lax.broadcasted_iota(jnp.int32, (64, 512), 1)
            g = gauss(i, j, s)
            hi, lo = split(g)
            hi_ref[pl.ds(at, 64), :] = hi
            lo_ref[pl.ds(at, 64), :] = lo
            if hi_ref is gxh:
                inv_x[pl.ds(at, 64), :] = jnp.broadcast_to(1.0 / jnp.sum(g, axis=1, keepdims=True), (64, 128))
                return total
            return total + jnp.sum(g, axis=0, keepdims=True)
        return lax.fori_loop(0, 8, tile, jnp.zeros((1, 512), F32))

    sum_y = wide(gyh, gyl, spread_ref[2])
    wide(gxh, gxl, spread_ref[1])

    def plane(q):
        return ((q >> 2) & 3) * 16 + (q >> 5) * 8 + (q & 3) * 2 + ((q >> 4) & 1)

    i = lax.broadcasted_iota(jnp.int32, (64, 192), 0)
    j = lax.broadcasted_iota(jnp.int32, (64, 192), 1)
    hi, lo = split(gauss(plane(i), plane(j & 63), spread_ref[0]))
    gz3[...] = jnp.where(j < 128, hi.astype(F32), lo.astype(F32)).astype(BF)

    planes = sp * 2 + lax.broadcasted_iota(jnp.int32, (8, 128), 0)
    others = lax.broadcasted_iota(jnp.int32, (8, 128), 1)
    near = jnp.where(others < 64, gauss(planes, others, spread_ref[0]), 0.0)
    sum_z = jnp.sum(near, axis=1, keepdims=True)

    fetch.wait()
    for p in range(2):
        inv_y = 1.0 / (sum_y * sum_z[p : p + 1, :])

        def first(m, carry):
            rows = pl.ds(pl.multiple_of(p * 512 + m * 64, 64), 64)
            inv = inv_x[pl.ds(pl.multiple_of(m * 64, 64), 64), :]
            hi, lo = split(dens_ref[rows, :] * jnp.concatenate([inv] * 4, axis=1) * inv_y)
            whi[rows, :] = hi
            wlo[rows, :] = lo
            return carry
        lax.fori_loop(0, 8, first, 0)

    pl.semaphore_wait(barrier, len(peers))

    sent = []
    outs = []
    count = [0]
    turn = [0]

    def remote(src, dst, to):
        n = count[0]
        count[0] += 1
        if len(sent) >= LIVE:
            sent.pop(0).wait_send()
        turn[0] = (turn[0] + 1) % LIVE
        copy = pltpu.make_async_remote_copy(
            src, dst, send_sem.at[turn[0]], recv_sem.at[n], device_id=to, device_id_type=MESH
        )
        copy.start()
        sent.append(copy)
        return copy.wait_recv

    def local(src, dst):
        n = count[0]
        count[0] += 1
        copy = pltpu.make_async_copy(src, dst, recv_sem.at[n])
        copy.start()
        return copy.wait

    pending = {}

    def finish(*key):
        for wait in pending.pop(key):
            wait()

    own_rows = pl.ds(pl.multiple_of(core * 8, 8), 8)
    other_rows = pl.ds(pl.multiple_of((1 - core) * 8, 8), 8)

    def slot(ref, lead, axis, k, rows):
        at = [slice(None)] * 4
        at["zpyx".index(axis)] = k
        return ref.at[(*lead, *at, rows)]

    def swap(src, s_lead, dst, d_lead, axis, rows, forward):
        waits = []
        for k in range(SIZE[axis]):
            to = around(axis, k)
            take, put = to, me[axis]
            if axis == "z":
                take, put = (lax.rem(eff + k, 2), zl) if forward else (to, eff)
            pair = slot(src, s_lead, axis, take, rows), slot(dst, d_lead, axis, put, rows)
            waits.append(remote(*pair, device(**{axis: to})) if k else local(*pair))
        return waits

    bufs = (b0, b1, b2)

    def start(a, j, c, u):
        rows = own_rows if u else other_rows
        pending["a2a", a, j, c, u] = swap(bufs[a], (j, c), bufs[a], (j + 1, c), AXES[a][c][u][j], rows, a != 1)

    wts[0] = jnp.full((8, 128), wt_ref[0], F32)
    pending["wc",] = [remote(wts.at[0], wts.at[1], device(k=1 - core))]

    def weights():
        finish("wc")
        wts[2] = wts[0] + wts[1]
        pending["wh",] = [
            remote(wts.at[2], wts.at[2 + k], device(h=lax.rem(zh + k, 4))) for k in range(1, 4)
        ]

    def total_weight():
        finish("wh")
        wts[6] = 1.0 / (wts[2] + wts[3] + (wts[4] + wts[5]))

    def step_adv(a, j, c, u):
        finish("a2a", a, j, c, u)
        start(a, j + 1, c, u)

    def step_conv(a, h):
        cols = slice(h * 256, h * 256 + 256)

        def along_y(m, carry):
            rows = pl.ds(pl.multiple_of(m * 256, 256), 256)
            x = dot(whi[rows, :], gyh[:, cols]) + (dot(wlo[rows, :], gyh[:, cols]) + dot(whi[rows, :], gyl[:, cols]))
            hi, lo = split(x)
            thi[rows, :] = hi
            tlo[rows, :] = lo
            return carry
        lax.fori_loop(0, 4, along_y, 0)

        for p in range(2):
            def along_x(m, carry):
                rows = pl.ds(pl.multiple_of(m * 128, 128), 128)
                k = slice(p * 512, p * 512 + 512)
                x = dot(gxh[rows, :], thi[k, :]) + (dot(gxl[rows, :], thi[k, :]) + dot(gxh[rows, :], tlo[k, :]))
                for e in range(2):
                    bufs[a][0, 2 * h + e, :, p, m] = x[:, e * 128 : e * 128 + 128].reshape(2, 4, 16, 128)
                return carry
            lax.fori_loop(0, 4, along_x, 0)
        for e in range(2):
            start(a, 0, 2 * h + e, 0)
            start(a, 0, 2 * h + e, 1)
        if a == 0 and h == 1:
            weights()

    def columns(x):
        hi, lo = split(x)
        return dot(gz3[...], jnp.concatenate([hi, lo, hi], axis=0))

    def convolved(a, c, first):
        flat = bufs[a].at[3, c].reshape(1024, 128)
        weight = wt_ref[0]

        def pair(n, carry):
            r = first + n * 2
            x = jnp.concatenate([flat[pl.ds(r + e, 64, stride=16), :] for e in range(2)], axis=1)
            y = columns(x)
            for e in range(2):
                part = y[:, e * 128 : e * 128 + 128]
                if a == 0:
                    d_ref[c, r + e] = part
                else:
                    part = d_ref[c, r + e] * part
                t_ref[a // 2, c, r + e] = weight * jnp.log(part)
            return carry
        lax.fori_loop(0, 4, pair, 0)

    def step_zo(a, c):
        ph = a // 2
        finish("a2a", a, 2, c, 0)
        convolved(a, c, (1 - core) * 8)
        pending["cs", ph, c] = [remote(t_ref.at[ph, c, other_rows], cb_ref.at[ph, c], device(k=1 - core))]

    def step_zw(a, c):
        finish("a2a", a, 2, c, 1)
        convolved(a, c, core * 8)

    mine = pl.ds(quarter * 2, 2)
    given = pl.ds(bit_one * 4 + (1 - bit_two) * 2, 2)
    half_mine = pl.ds(bit_one * 4, 4)
    half_given = pl.ds((1 - bit_one) * 4, 4)

    def step_cs(a, c):
        ph = a // 2
        finish("cs", ph, c)
        u_ref[ph, c] = t_ref[ph, c, own_rows] + cb_ref[ph, c]
        pending["rs1", ph, c] = [remote(u_ref.at[ph, c, half_given], r1_ref.at[ph, c], one)]

    def step_rs1(a, c):
        ph = a // 2
        finish("rs1", ph, c)
        u_ref[ph, c, half_mine] += r1_ref[ph, c]
        pending["rs2", ph, c] = [remote(u_ref.at[ph, c, given], r2_ref.at[ph, c], two)]

    def step_rs2(a, c):
        ph = a // 2
        if ("wh",) in pending:
            total_weight()
        finish("rs2", ph, c)
        total = u_ref[ph, c, mine] + r2_ref[ph, c]
        mean = jnp.exp(total * wts[6, 0:1, 0:1].reshape(1, 1, 1))
        if a == 0:
            bar_ref[c, mine] = mean
            here = bar_ref.at[c, mine]
            pending["ag1", c] = [remote(here, here, two)]
        else:
            flat = share_ref.at[0].reshape(512, 128)
            for e in range(2):
                flat[pl.ds(c * 2 + e, 64, stride=8), :] = mean[e]

    def step_ag1(a, c):
        finish("ag1", c)
        here = bar_ref.at[c, half_mine]
        pending["ag2", c] = [remote(here, here, one)]

    def step_ag2(a, c):
        finish("ag2", c)
        pending["cg", c] = [remote(bar_ref.at[c], oth_ref.at[c], device(k=1 - core))]

    def scaled(src, c, first):
        flat = b1.at[0, c].reshape(1024, 128)

        def pair(n, carry):
            r = first + n * 2
            parts = []
            for e in range(2):
                v = src[c, n * 2 + e] / d_ref[c, r + e]
                d_ref[c, r + e] = v
                parts.append(v)
            y = columns(jnp.concatenate(parts, axis=1))
            for e in range(2):
                flat[pl.ds(r + e, 64, stride=16), :] = y[:, e * 128 : e * 128 + 128]
            return carry
        lax.fori_loop(0, 4, pair, 0)

    def step_zbw(a, c):
        scaled(bar_ref, c, core * 8)
        start(1, 0, c, 1)

    def step_zbo(a, c):
        finish("cg", c)
        scaled(oth_ref, c, (1 - core) * 8)
        start(1, 0, c, 0)

    def step_xb(h):
        for e in range(2):
            finish("a2a", 1, 2, 2 * h + e, 0)
            finish("a2a", 1, 2, 2 * h + e, 1)
        cols = slice(h * 256, h * 256 + 256)
        for p in range(2):
            x = jnp.concatenate(
                [
                    jnp.concatenate([b1[3, 2 * h + e, k % 2, p, k // 2].reshape(64, 128) for k in range(8)], axis=0)
                    for e in range(2)
                ],
                axis=1,
            )
            hi, lo = split(x)
            thi[p * 512 : p * 512 + 512, :] = hi
            tlo[p * 512 : p * 512 + 512, :] = lo

            def along_x(m, carry):
                rows = pl.ds(pl.multiple_of(m * 128, 128), 128)
                to = pl.ds(pl.multiple_of(p * 512 + m * 128, 128), 128)
                k = slice(p * 512, p * 512 + 512)
                x = dot(gxh[rows, :], thi[k, :]) + (dot(gxl[rows, :], thi[k, :]) + dot(gxh[rows, :], tlo[k, :]))
                hi, lo = split(x)
                whi[to, cols] = hi
                wlo[to, cols] = lo
                return carry
            lax.fori_loop(0, 4, along_x, 0)

    def step_yb():
        def along_y(m, carry):
            rows = pl.ds(pl.multiple_of(m * 128, 128), 128)
            a_hi, a_lo = whi[rows, :], wlo[rows, :]
            x = dot(a_hi, gyh[...]) + (dot(a_lo, gyh[...]) + dot(a_hi, gyl[...]))
            w = dens_ref[rows, :] / x
            w_ref[rows, :] = w
            hi, lo = split(w)
            whi[rows, :] = hi
            wlo[rows, :] = lo
            return carry
        lax.fori_loop(0, 8, along_y, 0)
        copy = pltpu.make_async_copy(w_ref, w_hbm, io_sem.at[1])
        copy.start()
        outs.append(copy)

    def part(ref, h):
        return ref.at[..., pl.ds(h * 4, 4), :]

    def step_tx(h):
        pending["tail", h] = swap(share_ref, (0,), share_ref, (1,), "x", pl.ds(h * 4, 4), False)

    def step_ty(h):
        finish("tail", h)
        pending["tail", h] = swap(share_ref, (1,), share_ref, (2,), "y", pl.ds(h * 4, 4), False)

    def step_tz(h):
        finish("tail", h)
        pending["tail", h] = swap(share_ref, (2,), gath_ref, (core, zh), "z", pl.ds(h * 4, 4), False)

    def both(to_right, to_left):
        return [remote(to_right, to_right, device(h=right)), remote(to_left, to_left, device(h=left))]

    def across(h, *at):
        here = part(gath_ref.at[(core,) + at], h)
        pending["over", h].append(remote(here, here, device(k=1 - core)))

    def step_tg(h):
        finish("tail", h)
        here = part(gath_ref.at[core, zh], h)
        pending["tail", h] = both(here, here)
        pending["over", h] = []
        across(h, zh)

    def step_th(h):
        finish("tail", h)
        pending["tail", h] = both(part(gath_ref.at[core, left, 0], h), part(gath_ref.at[core, right, 1], h))
        across(h, left)
        across(h, right)

    def step_ti(h):
        finish("tail", h)
        across(h, far)

    def step_tp(h):
        def place(k):
            for h_from in range(NHD):
                for z in range(2):
                    src = gath_ref.at[k, h_from, z].reshape(256, 128)
                    bits = h_from // 2, (h_from + h_from // 2) % 2
                    row = bits[z] * 4 + bits[1 - z] * 2
                    for c in (2 * h, 2 * h + 1):
                        dst = bary_ref.at[c, z]
                        for e in range(2):
                            dst[pl.ds(k * 8 + row + e, 32, stride=16), :] = src[pl.ds(c * 2 + e, 32, stride=8), :]

        place(core)
        finish("over", h)
        place(1 - core)
        for c in (2 * h, 2 * h + 1):
            for z in range(2):
                copy = pltpu.make_async_copy(
                    bary_ref.at[c, z].reshape(8, 64, 128), bary_hbm.at[:, z, :, pl.ds(c * 128, 128)], io_sem.at[2 + 2 * c + z]
                )
                copy.start()
                outs.append(copy)

    table = {
        "conv": step_conv, "adv": step_adv, "zo": step_zo, "zw": step_zw, "cs": step_cs, "rs1": step_rs1, "rs2": step_rs2,
        "ag1": step_ag1, "ag2": step_ag2, "zbw": step_zbw, "zbo": step_zbo, "xb": step_xb, "yb": step_yb,
        "tx": step_tx, "ty": step_ty, "tz": step_tz, "tg": step_tg, "th": step_th, "ti": step_ti, "tp": step_tp,
    }
    for name, *rest in ORDER:
        table[name](*rest)
    for copy in sent:
        copy.wait_send()
    for copy in outs:
        copy.wait()
    assert count[0] <= SEMS and not pending


SEMS = 330
LIVE = 100


def local(densities, weights, spreads):
    field = (4, CH, 2, 2, 4, 4, 16, 128)
    vmem = pltpu.VMEM
    scratch = [
        vmem((1024, 512), F32), vmem((1024, 512), F32), vmem((CH, 2, 512, 128), F32), vmem((512, 128), F32),
        vmem(field, F32), vmem(field, F32), vmem(field, F32),
        vmem((CH, 16, 64, 128), F32),
        vmem((2, CH, 16, 64, 128), F32),
        vmem((2, CH, 8, 64, 128), F32),
        vmem((2, CH, 8, 64, 128), F32),
        vmem((2, CH, 4, 64, 128), F32),
        vmem((2, CH, 2, 64, 128), F32),
        vmem((CH, 8, 64, 128), F32),
        vmem((CH, 8, 64, 128), F32),
        vmem((3, 2, 2, 4, 4, 8, 128), F32),
        vmem((2, 4, 2, 2, 4, 4, 8, 128), F32),
        vmem((1024, 512), BF), vmem((1024, 512), BF),
        vmem((1024, 256), BF), vmem((1024, 256), BF),
        vmem((512, 512), BF), vmem((512, 512), BF), vmem((512, 512), BF), vmem((512, 512), BF),
        vmem((64, 192), BF),
        vmem((7, 8, 128), F32),
        pltpu.SemaphoreType.DMA((10,)), pltpu.SemaphoreType.DMA((LIVE,)), pltpu.SemaphoreType.DMA((SEMS,)),
    ]
    whole = pl.BlockSpec(memory_space=pl.ANY)
    smem = pl.BlockSpec(memory_space=pltpu.SMEM)
    bary, scale_w = pl.pallas_call(
        body,
        out_shape=[
            jax.ShapeDtypeStruct((8, 2, 64, 512), F32),
            jax.ShapeDtypeStruct((1024, 512), F32),
        ],
        in_specs=[whole, smem, smem],
        out_specs=[whole, whole],
        scratch_shapes=scratch,
        compiler_params=pltpu.CompilerParams(
            collective_id=0, has_side_effects=True, vmem_limit_bytes=61 * 1024 * 1024
        ),
        name="sinkhorn",
    )(densities.reshape(1024, 512), weights, spreads)
    return bary.reshape(2, 512, 512), scale_w.reshape(1, 2, 512, 512)


def solution(mesh):
    return jax.shard_map(
        local,
        mesh=mesh,
        in_specs=(P("dens", "sp", None, None), P("dens"), P()),
        out_specs=(P("sp", None, None), P("dens", "sp", None, None)),
        check_vma=False,
    )
```

time: 207 us -> 196 us (0.947)
  Pallas kernels: 201 us -> 190 us
    pallas_call x1, Pallas kernels: 201 us -> 190 us  [local(): pl.pallas_call(body, out_shape=[jax.ShapeDtypeStruct((8, 2, 64, 512), F32...]
where the time goes in v3:
time: 196 us; the launch traced here: 195 us
  Pallas kernels  190 us (97%)
  local copies, waits for them, and re-layouts  4.55 us (2%)
    pallas_call x1, Pallas kernels, local(): pl.pallas_call(body, out_shape=[jax.ShapeDtypeStruct((8, 2, 64, 512), F32...  190 us
    unnamed x4, local copies, waits for them, and re-layouts  4.55 us

profile of v3, /device:TPU:1, one launch (start us, length us, event | category | flops | bytes accessed | tf_op | source)
XLA Modules:
  0.0 195.4 jit_solution(8754688301231689077)
XLA Ops:
  1.3 189.6 %sinkhorn.1 = (f32[8,2,64,512]{3,2,1,0:T(8,128)}, f32[1024,512]{1,0:T(8,128)}) custom-call(f32[1024,512]{1,0:T(8,128)} %bitcast.3, f32[1]{0:T(128)S(6)} %copy.7.wt_ref, f32[3]{0:T(128)} %spread_ref.1), custom_call_target="tpu_custom_call" | custom-call | tf_op jit(solution)/shard_map/sinkhorn/pallas_call | solution.py:492
  190.9 0.0 copy-start
  190.9 3.2 %copy.8 = f32[2,512,512]{2,1,0:T(8,128)} copy(f32[2,512,512]{2,1,0:T(8,128)} %bitcast.5) | data formatting | bytes 4194304
  194.1 0.0 copy-done
  194.1 1.3 copy.9
Async XLA Ops:
  190.9 3.2 %copy-start = (f32[1024,512]{1,0:T(8,128)S(1)}, f32[1024,512]{1,0:T(8,128)}, u32[]{:S(2)}) copy-start(f32[1024,512]{1,0:T(8,128)} %get-tuple-element.5) | copy-start | bytes 6291460

commit v4 on v3

--- a/solution.py
+++ b/solution.py
@@ -1,4 +1,4 @@
-import functools
+import itertools
 import math
 
 import jax
@@ -16,31 +16,26 @@
 CH = 4
 SIZE = {"x": NXD, "y": NYD, "z": NZD}
 AXES = (
-    (("yxz", "yzx"), ("zyx", "xzy"), ("yxz", "zyx"), ("xyz", "yzx")),
-    (("zyx", "xyz"), ("yxz", "xyz"), ("xzy", "zyx"), ("xyz", "zxy")),
-    (("yzx", "yzx"), ("zxy", "xyz"), ("xzy", "xzy"), ("yzx", "yxz")),
+    ((("x", "yz"), ("x", "yz")), (("x", "yz"), ("yz", "x")), (("yz", "x"), ("x", "yz")), (("x", "yz"), ("x", "yz"))),
+    ((("x", "yz"), ("x", "yz")), (("x", "yz"), ("x", "yz")), (("x", "yz"), ("yz", "x")), (("x", "yz"), ("yz", "x"))),
+    ((("yz", "x"), ("yz", "x")), (("yz", "x"), ("x", "yz")), (("yz", "x"), ("x", "yz")), (("yz", "x"), ("yz", "x"))),
 )
 
 
 ORDER = (
-    ("conv", 0, 0), ("conv", 0, 1), ("adv", 0, 0, 0, 0), ("adv", 0, 0, 1, 0), ("adv", 0, 0, 1, 1), ("adv", 0, 0, 0, 1),
-    ("adv", 0, 0, 2, 1), ("adv", 0, 0, 3, 0), ("adv", 0, 0, 2, 0), ("adv", 0, 1, 0, 0), ("adv", 0, 1, 1, 1), ("adv", 0, 0, 3, 1),
-    ("adv", 0, 1, 0, 1), ("adv", 0, 1, 2, 0), ("adv", 0, 1, 1, 0), ("zo", 0, 0), ("adv", 0, 1, 2, 1), ("zw", 0, 0),
-    ("adv", 0, 1, 3, 1), ("cs", 0, 0), ("adv", 0, 1, 3, 0), ("zo", 0, 1), ("zo", 0, 2), ("zw", 0, 1), ("zw", 0, 2), ("cs", 0, 1),
-    ("rs1", 0, 0), ("cs", 0, 2), ("zo", 0, 3), ("zw", 0, 3), ("cs", 0, 3), ("rs1", 0, 1), ("rs2", 0, 0), ("rs1", 0, 2),
-    ("rs1", 0, 3), ("rs2", 0, 1), ("ag1", 0, 0), ("rs2", 0, 2), ("rs2", 0, 3), ("ag1", 0, 1), ("ag2", 0, 0), ("zbw", 0, 0),
-    ("ag1", 0, 2), ("ag1", 0, 3), ("zbo", 0, 0), ("ag2", 0, 1), ("zbw", 0, 1), ("adv", 1, 0, 0, 1), ("ag2", 0, 2), ("zbw", 0, 2),
-    ("zbo", 0, 1), ("adv", 1, 0, 0, 0), ("ag2", 0, 3), ("zbw", 0, 3), ("zbo", 0, 2), ("adv", 1, 0, 1, 1), ("adv", 1, 1, 0, 1),
-    ("zbo", 0, 3), ("adv", 1, 0, 2, 1), ("adv", 1, 0, 1, 0), ("adv", 1, 0, 3, 1), ("adv", 1, 0, 2, 0), ("adv", 1, 1, 0, 0),
-    ("adv", 1, 0, 3, 0), ("adv", 1, 1, 1, 1), ("adv", 1, 1, 2, 0), ("adv", 1, 1, 1, 0), ("adv", 1, 1, 2, 1), ("adv", 1, 1, 3, 0),
-    ("adv", 1, 1, 3, 1), ("xb", 0), ("xb", 1), ("yb",), ("conv", 2, 0), ("conv", 2, 1), ("adv", 2, 0, 0, 0), ("adv", 2, 0, 1, 0),
-    ("adv", 2, 0, 1, 1), ("adv", 2, 0, 0, 1), ("adv", 2, 0, 2, 0), ("adv", 2, 1, 0, 0), ("adv", 2, 0, 2, 1), ("adv", 2, 0, 3, 0),
-    ("adv", 2, 1, 0, 1), ("adv", 2, 0, 3, 1), ("adv", 2, 1, 1, 0), ("adv", 2, 1, 2, 0), ("adv", 2, 1, 1, 1), ("zo", 2, 0),
-    ("adv", 2, 1, 2, 1), ("zw", 2, 0), ("zo", 2, 1), ("cs", 2, 0), ("adv", 2, 1, 3, 0), ("adv", 2, 1, 3, 1), ("zo", 2, 2),
-    ("zw", 2, 1), ("zw", 2, 2), ("cs", 2, 1), ("cs", 2, 2), ("rs1", 2, 0), ("zo", 2, 3), ("zw", 2, 3), ("cs", 2, 3),
-    ("rs1", 2, 1), ("rs1", 2, 2), ("rs2", 2, 0), ("rs1", 2, 3), ("rs2", 2, 1), ("tx", 0), ("rs2", 2, 2), ("rs2", 2, 3), ("tx", 1),
-    ("ty", 0), ("ty", 1), ("tz", 0), ("tz", 1), ("tg", 0), ("tg", 1), ("th", 0), ("th", 1), ("ti", 0), ("ti", 1), ("tp", 0),
-    ("tp", 1),
+    ("conv", 0, 0), ("conv", 0, 1), ("adv", 0, 0, 0, 0), ("adv", 0, 0, 1, 1), ("adv", 0, 0, 0, 1), ("adv", 0, 0, 2, 0),
+    ("adv", 0, 0, 1, 0), ("zo", 0, 0), ("adv", 0, 0, 2, 1), ("zw", 0, 0), ("cs", 0, 0), ("adv", 0, 0, 3, 0), ("zo", 0, 1),
+    ("adv", 0, 0, 3, 1), ("zw", 0, 2), ("rs1", 0, 0), ("zw", 0, 1), ("zo", 0, 3), ("cs", 0, 1), ("zo", 0, 2), ("zw", 0, 3),
+    ("rs2", 0, 0), ("cs", 0, 3), ("cs", 0, 2), ("rs1", 0, 1), ("ag1", 0, 0), ("rs1", 0, 3), ("rs1", 0, 2), ("rs2", 0, 1),
+    ("ag2", 0, 0), ("zbw", 0, 0), ("rs2", 0, 3), ("rs2", 0, 2), ("zbo", 0, 0), ("ag1", 0, 1), ("ag1", 0, 3), ("adv", 1, 0, 0, 1),
+    ("ag1", 0, 2), ("adv", 1, 0, 0, 0), ("ag2", 0, 1), ("zbw", 0, 1), ("ag2", 0, 3), ("zbw", 0, 3), ("zbo", 0, 1), ("ag2", 0, 2),
+    ("zbw", 0, 2), ("zbo", 0, 3), ("adv", 1, 0, 1, 1), ("zbo", 0, 2), ("adv", 1, 0, 3, 1), ("adv", 1, 0, 1, 0),
+    ("adv", 1, 0, 2, 1), ("adv", 1, 0, 3, 0), ("adv", 1, 0, 2, 0), ("xb", 0), ("xb", 1), ("yb",), ("conv", 2, 0), ("conv", 2, 1),
+    ("adv", 2, 0, 0, 0), ("adv", 2, 0, 1, 1), ("adv", 2, 0, 0, 1), ("adv", 2, 0, 2, 1), ("adv", 2, 0, 1, 0), ("zo", 2, 0),
+    ("adv", 2, 0, 2, 0), ("zw", 2, 0), ("cs", 2, 0), ("adv", 2, 0, 3, 0), ("zo", 2, 1), ("adv", 2, 0, 3, 1), ("zo", 2, 2),
+    ("rs1", 2, 0), ("zw", 2, 1), ("zo", 2, 3), ("cs", 2, 1), ("zw", 2, 2), ("zw", 2, 3), ("cs", 2, 2), ("rs2", 2, 0),
+    ("cs", 2, 3), ("rs1", 2, 1), ("rs1", 2, 2), ("rs1", 2, 3), ("rs2", 2, 1), ("tx", 0), ("rs2", 2, 2), ("rs2", 2, 3), ("tx", 1),
+    ("ty", 0), ("ty", 1), ("tg", 0), ("tg", 1), ("th", 0), ("th", 1), ("ti", 0), ("ti", 1), ("tp", 0), ("tp", 1),
 )
 
 
@@ -81,6 +76,7 @@
     bit_two = gray * (1 - eff) + (zh // 2) * eff
     quarter = bit_one * 2 + bit_two
     peers = [device(**{axis: around(axis, k)}) for axis in "xyz" for k in range(1, SIZE[axis])]
+    peers += [device(y=around("y", k), z=around("z", 1)) for k in range(1, NYD)]
     peers += [device(k=1 - core), device(h=right), device(h=left), device(h=far), one, two]
 
     barrier = pltpu.get_barrier_semaphore()
@@ -175,27 +171,31 @@
     own_rows = pl.ds(pl.multiple_of(core * 8, 8), 8)
     other_rows = pl.ds(pl.multiple_of((1 - core) * 8, 8), 8)
 
-    def slot(ref, lead, axis, k, rows):
-        at = [slice(None)] * 4
-        at["zpyx".index(axis)] = k
-        return ref.at[(*lead, *at, rows)]
-
-    def swap(src, s_lead, dst, d_lead, axis, rows, forward):
+    def slot(ref, lead, at, rows):
+        at = tuple(at.get(axis, slice(None)) for axis in "zpyx")
+        return ref.at[(*lead, *at) if rows is None else (*lead, *at, rows)]
+
+    def swap(src, s_lead, dst, d_lead, axes, rows, forward):
         waits = []
-        for k in range(SIZE[axis]):
-            to = around(axis, k)
-            take, put = to, me[axis]
-            if axis == "z":
-                take, put = (lax.rem(eff + k, 2), zl) if forward else (to, eff)
-            pair = slot(src, s_lead, axis, take, rows), slot(dst, d_lead, axis, put, rows)
-            waits.append(remote(*pair, device(**{axis: to})) if k else local(*pair))
+        for ks in itertools.product(*(range(SIZE[axis]) for axis in axes)):
+            to = {axis: around(axis, k) for axis, k in zip(axes, ks)}
+            take, put = dict(to), {axis: me[axis] for axis in axes}
+            if "z" in axes:
+                if forward:
+                    take["z"] = lax.rem(eff + ks[axes.index("z")], 2)
+                else:
+                    put["z"] = eff
+            pair = slot(src, s_lead, take, rows), slot(dst, d_lead, put, rows)
+            waits.append(remote(*pair, device(**to)) if any(ks) else local(*pair))
         return waits
 
     bufs = (b0, b1, b2)
 
     def start(a, j, c, u):
-        rows = own_rows if u else other_rows
-        pending["a2a", a, j, c, u] = swap(bufs[a], (j, c), bufs[a], (j + 1, c), AXES[a][c][u][j], rows, a != 1)
+        half = core if u else 1 - core
+        pending["a2a", a, j, c, u] = swap(
+            bufs[a], (j, c, half), bufs[a], (j + 1, c, half), AXES[a][c][u][j], None, a != 1
+        )
 
     wts[0] = jnp.full((8, 128), wt_ref[0], F32)
     pending["wc",] = [remote(wts.at[0], wts.at[1], device(k=1 - core))]
@@ -233,7 +233,9 @@
                 k = slice(p * 512, p * 512 + 512)
                 x = dot(gxh[rows, :], thi[k, :]) + (dot(gxl[rows, :], thi[k, :]) + dot(gxh[rows, :], tlo[k, :]))
                 for e in range(2):
-                    bufs[a][0, 2 * h + e, :, p, m] = x[:, e * 128 : e * 128 + 128].reshape(2, 4, 16, 128)
+                    block = x[:, e * 128 : e * 128 + 128].reshape(2, 4, 2, 8, 128)
+                    for half in range(2):
+                        bufs[a][0, 2 * h + e, half, :, p, m] = block[:, :, half]
                 return carry
             lax.fori_loop(0, 4, along_x, 0)
         for e in range(2):
@@ -246,13 +248,13 @@
         hi, lo = split(x)
         return dot(gz3[...], jnp.concatenate([hi, lo, hi], axis=0))
 
-    def convolved(a, c, first):
-        flat = bufs[a].at[3, c].reshape(1024, 128)
+    def convolved(a, c, half):
+        flat = bufs[a].at[2, c, half].reshape(512, 128)
         weight = wt_ref[0]
 
         def pair(n, carry):
-            r = first + n * 2
-            x = jnp.concatenate([flat[pl.ds(r + e, 64, stride=16), :] for e in range(2)], axis=1)
+            r = half * 8 + n * 2
+            x = jnp.concatenate([flat[pl.ds(n * 2 + e, 64, stride=8), :] for e in range(2)], axis=1)
             y = columns(x)
             for e in range(2):
                 part = y[:, e * 128 : e * 128 + 128]
@@ -266,13 +268,13 @@
 
     def step_zo(a, c):
         ph = a // 2
-        finish("a2a", a, 2, c, 0)
-        convolved(a, c, (1 - core) * 8)
+        finish("a2a", a, 1, c, 0)
+        convolved(a, c, 1 - core)
         pending["cs", ph, c] = [remote(t_ref.at[ph, c, other_rows], cb_ref.at[ph, c], device(k=1 - core))]
 
     def step_zw(a, c):
-        finish("a2a", a, 2, c, 1)
-        convolved(a, c, core * 8)
+        finish("a2a", a, 1, c, 1)
+        convolved(a, c, core)
 
     mine = pl.ds(quarter * 2, 2)
     given = pl.ds(bit_one * 4 + (1 - bit_two) * 2, 2)
@@ -316,11 +318,11 @@
         finish("ag2", c)
         pending["cg", c] = [remote(bar_ref.at[c], oth_ref.at[c], device(k=1 - core))]
 
-    def scaled(src, c, first):
-        flat = b1.at[0, c].reshape(1024, 128)
+    def scaled(src, c, half):
+        flat = b1.at[0, c, half].reshape(512, 128)
 
         def pair(n, carry):
-            r = first + n * 2
+            r = half * 8 + n * 2
             parts = []
             for e in range(2):
                 v = src[c, n * 2 + e] / d_ref[c, r + e]
@@ -328,31 +330,31 @@
                 parts.append(v)
             y = columns(jnp.concatenate(parts, axis=1))
             for e in range(2):
-                flat[pl.ds(r + e, 64, stride=16), :] = y[:, e * 128 : e * 128 + 128]
+                flat[pl.ds(n * 2 + e, 64, stride=8), :] = y[:, e * 128 : e * 128 + 128]
             return carry
         lax.fori_loop(0, 4, pair, 0)
 
     def step_zbw(a, c):
-        scaled(bar_ref, c, core * 8)
+        scaled(bar_ref, c, core)
         start(1, 0, c, 1)
 
     def step_zbo(a, c):
         finish("cg", c)
-        scaled(oth_ref, c, (1 - core) * 8)
+        scaled(oth_ref, c, 1 - core)
         start(1, 0, c, 0)
 
     def step_xb(h):
         for e in range(2):
-            finish("a2a", 1, 2, 2 * h + e, 0)
-            finish("a2a", 1, 2, 2 * h + e, 1)
+            finish("a2a", 1, 1, 2 * h + e, 0)
+            finish("a2a", 1, 1, 2 * h + e, 1)
         cols = slice(h * 256, h * 256 + 256)
         for p in range(2):
+            def block(c, k):
+                halves = [b1[2, c, half, k % 2, p, k // 2][:, None] for half in range(2)]
+                return jnp.concatenate(halves, axis=1).reshape(64, 128)
+
             x = jnp.concatenate(
-                [
-                    jnp.concatenate([b1[3, 2 * h + e, k % 2, p, k // 2].reshape(64, 128) for k in range(8)], axis=0)
-                    for e in range(2)
-                ],
-                axis=1,
+                [jnp.concatenate([block(2 * h + e, k) for k in range(8)], axis=0) for e in range(2)], axis=1
             )
             hi, lo = split(x)
             thi[p * 512 : p * 512 + 512, :] = hi
@@ -393,11 +395,7 @@
 
     def step_ty(h):
         finish("tail", h)
-        pending["tail", h] = swap(share_ref, (1,), share_ref, (2,), "y", pl.ds(h * 4, 4), False)
-
-    def step_tz(h):
-        finish("tail", h)
-        pending["tail", h] = swap(share_ref, (2,), gath_ref, (core, zh), "z", pl.ds(h * 4, 4), False)
+        pending["tail", h] = swap(share_ref, (1,), gath_ref, (core, zh), "yz", pl.ds(h * 4, 4), False)
 
     def both(to_right, to_left):
         return [remote(to_right, to_right, device(h=right)), remote(to_left, to_left, device(h=left))]
@@ -449,7 +447,7 @@
     table = {
         "conv": step_conv, "adv": step_adv, "zo": step_zo, "zw": step_zw, "cs": step_cs, "rs1": step_rs1, "rs2": step_rs2,
         "ag1": step_ag1, "ag2": step_ag2, "zbw": step_zbw, "zbo": step_zbo, "xb": step_xb, "yb": step_yb,
-        "tx": step_tx, "ty": step_ty, "tz": step_tz, "tg": step_tg, "th": step_th, "ti": step_ti, "tp": step_tp,
+        "tx": step_tx, "ty": step_ty, "tg": step_tg, "th": step_th, "ti": step_ti, "tp": step_tp,
     }
     for name, *rest in ORDER:
         table[name](*rest)
@@ -460,12 +458,12 @@
     assert count[0] <= SEMS and not pending
 
 
-SEMS = 330
+SEMS = 384
 LIVE = 100
 
 
 def local(densities, weights, spreads):
-    field = (4, CH, 2, 2, 4, 4, 16, 128)
+    field = (3, CH, 2, 2, 2, 4, 4, 8, 128)
     vmem = pltpu.VMEM
     scratch = [
         vmem((1024, 512), F32), vmem((1024, 512), F32), vmem((CH, 2, 512, 128), F32), vmem((512, 128), F32),
@@ -478,7 +476,7 @@
         vmem((2, CH, 2, 64, 128), F32),
         vmem((CH, 8, 64, 128), F32),
         vmem((CH, 8, 64, 128), F32),
-        vmem((3, 2, 2, 4, 4, 8, 128), F32),
+        vmem((2, 2, 2, 4, 4, 8, 128), F32),
         vmem((2, 4, 2, 2, 4, 4, 8, 128), F32),
         vmem((1024, 512), BF), vmem((1024, 512), BF),
         vmem((1024, 256), BF), vmem((1024, 256), BF),

time: 196 us -> 182 us (0.929)
  Pallas kernels: 190 us -> 174 us
    pallas_call x1, Pallas kernels: 190 us -> 174 us  [local(): pl.pallas_call(body, out_shape=[jax.ShapeDtypeStruct((8, 2, 64, 512), F32...]
where the time goes in v4:
time: 182 us; the launch traced here: 180 us
  Pallas kernels  174 us (96%)
  local copies, waits for them, and re-layouts  4.55 us (2%)
    pallas_call x1, Pallas kernels, local(): pl.pallas_call(body, out_shape=[jax.ShapeDtypeStruct((8, 2, 64, 512), F32...  174 us
    unnamed x4, local copies, waits for them, and re-layouts  4.55 us

profile of v4, /device:TPU:1, one launch (start us, length us, event | category | flops | bytes accessed | tf_op | source)
XLA Modules:
  0.0 180.2 jit_solution(15858846551938356362)
XLA Ops:
  1.3 174.3 %sinkhorn.1 = (f32[8,2,64,512]{3,2,1,0:T(8,128)}, f32[1024,512]{1,0:T(8,128)}) custom-call(f32[1024,512]{1,0:T(8,128)} %bitcast.3, f32[1]{0:T(128)S(6)} %copy.7.wt_ref, f32[3]{0:T(128)} %spread_ref.1), custom_call_target="tpu_custom_call" | custom-call | tf_op jit(solution)/shard_map/sinkhorn/pallas_call | solution.py:490
  175.6 0.0 copy-start
  175.6 3.2 %copy.8 = f32[2,512,512]{2,1,0:T(8,128)} copy(f32[2,512,512]{2,1,0:T(8,128)} %bitcast.5) | data formatting | bytes 4194304
  178.9 0.0 copy-done
  178.9 1.3 copy.9
Async XLA Ops:
  175.6 3.2 %copy-start = (f32[1024,512]{1,0:T(8,128)S(1)}, f32[1024,512]{1,0:T(8,128)}, u32[]{:S(2)}) copy-start(f32[1024,512]{1,0:T(8,128)} %get-tuple-element.5) | copy-start | bytes 6291460

commit v5 on v4

--- a/solution.py
+++ b/solution.py
@@ -30,7 +30,7 @@
     ("ag2", 0, 0), ("zbw", 0, 0), ("rs2", 0, 3), ("rs2", 0, 2), ("zbo", 0, 0), ("ag1", 0, 1), ("ag1", 0, 3), ("adv", 1, 0, 0, 1),
     ("ag1", 0, 2), ("adv", 1, 0, 0, 0), ("ag2", 0, 1), ("zbw", 0, 1), ("ag2", 0, 3), ("zbw", 0, 3), ("zbo", 0, 1), ("ag2", 0, 2),
     ("zbw", 0, 2), ("zbo", 0, 3), ("adv", 1, 0, 1, 1), ("zbo", 0, 2), ("adv", 1, 0, 3, 1), ("adv", 1, 0, 1, 0),
-    ("adv", 1, 0, 2, 1), ("adv", 1, 0, 3, 0), ("adv", 1, 0, 2, 0), ("xb", 0), ("xb", 1), ("yb",), ("conv", 2, 0), ("conv", 2, 1),
+    ("adv", 1, 0, 2, 1), ("adv", 1, 0, 3, 0), ("adv", 1, 0, 2, 0), ("xb", 0), ("ya",), ("xb", 1), ("yb",), ("conv", 2, 0), ("conv", 2, 1),
     ("adv", 2, 0, 0, 0), ("adv", 2, 0, 1, 1), ("adv", 2, 0, 0, 1), ("adv", 2, 0, 2, 1), ("adv", 2, 0, 1, 0), ("zo", 2, 0),
     ("adv", 2, 0, 2, 0), ("zw", 2, 0), ("cs", 2, 0), ("adv", 2, 0, 3, 0), ("zo", 2, 1), ("adv", 2, 0, 3, 1), ("zo", 2, 2),
     ("rs1", 2, 0), ("zw", 2, 1), ("zo", 2, 3), ("cs", 2, 1), ("zw", 2, 2), ("zw", 2, 3), ("cs", 2, 2), ("rs2", 2, 0),
@@ -371,12 +371,21 @@
                 return carry
             lax.fori_loop(0, 4, along_x, 0)
 
+    def over_lanes(rows, cols):
+        a_hi, a_lo = whi[rows, cols], wlo[rows, cols]
+        return dot(a_hi, gyh[cols, :]) + (dot(a_lo, gyh[cols, :]) + dot(a_hi, gyl[cols, :]))
+
+    def step_ya():
+        def along_y(m, carry):
+            rows = pl.ds(pl.multiple_of(m * 128, 128), 128)
+            w_ref[rows, :] = over_lanes(rows, slice(0, 256))
+            return carry
+        lax.fori_loop(0, 8, along_y, 0)
+
     def step_yb():
         def along_y(m, carry):
             rows = pl.ds(pl.multiple_of(m * 128, 128), 128)
-            a_hi, a_lo = whi[rows, :], wlo[rows, :]
-            x = dot(a_hi, gyh[...]) + (dot(a_lo, gyh[...]) + dot(a_hi, gyl[...]))
-            w = dens_ref[rows, :] / x
+            w = dens_ref[rows, :] / (w_ref[rows, :] + over_lanes(rows, slice(256, 512)))
             w_ref[rows, :] = w
             hi, lo = split(w)
             whi[rows, :] = hi
@@ -446,7 +455,7 @@
 
     table = {
         "conv": step_conv, "adv": step_adv, "zo": step_zo, "zw": step_zw, "cs": step_cs, "rs1": step_rs1, "rs2": step_rs2,
-        "ag1": step_ag1, "ag2": step_ag2, "zbw": step_zbw, "zbo": step_zbo, "xb": step_xb, "yb": step_yb,
+        "ag1": step_ag1, "ag2": step_ag2, "zbw": step_zbw, "zbo": step_zbo, "xb": step_xb, "ya": step_ya, "yb": step_yb,
         "tx": step_tx, "ty": step_ty, "tg": step_tg, "th": step_th, "ti": step_ti, "tp": step_tp,
     }
     for name, *rest in ORDER:

time: 182 us -> 181 us (level)
  no operation moved by 1% of the time
where the time goes in v5:
time: 181 us
  Pallas kernels  175 us (97%)
  local copies, waits for them, and re-layouts  4.55 us (3%)
    pallas_call x1, Pallas kernels, local(): pl.pallas_call(body, out_shape=[jax.ShapeDtypeStruct((8, 2, 64, 512), F32...  175 us
    unnamed x4, local copies, waits for them, and re-layouts  4.55 us

profile of v5, /device:TPU:1, one launch (start us, length us, event | category | flops | bytes accessed | tf_op | source)
XLA Modules:
  0.0 180.9 jit_solution(5668688836913873742)
XLA Ops:
  1.3 175.1 %sinkhorn.1 = (f32[8,2,64,512]{3,2,1,0:T(8,128)}, f32[1024,512]{1,0:T(8,128)}) custom-call(f32[1024,512]{1,0:T(8,128)} %bitcast.3, f32[1]{0:T(128)S(6)} %copy.7.wt_ref, f32[3]{0:T(128)} %spread_ref.1), custom_call_target="tpu_custom_call" | custom-call | tf_op jit(solution)/shard_map/sinkhorn/pallas_call | solution.py:499
  176.4 0.0 copy-start
  176.4 3.2 %copy.8 = f32[2,512,512]{2,1,0:T(8,128)} copy(f32[2,512,512]{2,1,0:T(8,128)} %bitcast.5) | data formatting | bytes 4194304
  179.6 0.0 copy-done
  179.6 1.3 copy.9
Async XLA Ops:
  176.4 3.2 %copy-start = (f32[1024,512]{1,0:T(8,128)S(1)}, f32[1024,512]{1,0:T(8,128)}, u32[]{:S(2)}) copy-start(f32[1024,512]{1,0:T(8,128)} %get-tuple-element.5) | copy-start | bytes 6291460

commit v6 on v5

--- a/solution.py
+++ b/solution.py
@@ -16,26 +16,26 @@
 CH = 4
 SIZE = {"x": NXD, "y": NYD, "z": NZD}
 AXES = (
-    ((("x", "yz"), ("x", "yz")), (("x", "yz"), ("yz", "x")), (("yz", "x"), ("x", "yz")), (("x", "yz"), ("x", "yz"))),
-    ((("x", "yz"), ("x", "yz")), (("x", "yz"), ("x", "yz")), (("x", "yz"), ("yz", "x")), (("x", "yz"), ("yz", "x"))),
-    ((("yz", "x"), ("yz", "x")), (("yz", "x"), ("x", "yz")), (("yz", "x"), ("x", "yz")), (("yz", "x"), ("yz", "x"))),
+    ((("x", "yz"), ("yz", "x")), (("yz", "x"), ("x", "yz")), (("x", "yz"), ("yz", "x")), (("yz", "x"), ("x", "yz"))),
+    ((("x", "yz"), ("yz", "x")), (("yz", "x"), ("x", "yz")), (("x", "yz"), ("yz", "x")), (("yz", "x"), ("x", "yz"))),
+    ((("x", "yz"), ("yz", "x")), (("yz", "x"), ("x", "yz")), (("x", "yz"), ("yz", "x")), (("yz", "x"), ("x", "yz"))),
 )
 
 
 ORDER = (
-    ("conv", 0, 0), ("conv", 0, 1), ("adv", 0, 0, 0, 0), ("adv", 0, 0, 1, 1), ("adv", 0, 0, 0, 1), ("adv", 0, 0, 2, 0),
-    ("adv", 0, 0, 1, 0), ("zo", 0, 0), ("adv", 0, 0, 2, 1), ("zw", 0, 0), ("cs", 0, 0), ("adv", 0, 0, 3, 0), ("zo", 0, 1),
-    ("adv", 0, 0, 3, 1), ("zw", 0, 2), ("rs1", 0, 0), ("zw", 0, 1), ("zo", 0, 3), ("cs", 0, 1), ("zo", 0, 2), ("zw", 0, 3),
-    ("rs2", 0, 0), ("cs", 0, 3), ("cs", 0, 2), ("rs1", 0, 1), ("ag1", 0, 0), ("rs1", 0, 3), ("rs1", 0, 2), ("rs2", 0, 1),
-    ("ag2", 0, 0), ("zbw", 0, 0), ("rs2", 0, 3), ("rs2", 0, 2), ("zbo", 0, 0), ("ag1", 0, 1), ("ag1", 0, 3), ("adv", 1, 0, 0, 1),
-    ("ag1", 0, 2), ("adv", 1, 0, 0, 0), ("ag2", 0, 1), ("zbw", 0, 1), ("ag2", 0, 3), ("zbw", 0, 3), ("zbo", 0, 1), ("ag2", 0, 2),
-    ("zbw", 0, 2), ("zbo", 0, 3), ("adv", 1, 0, 1, 1), ("zbo", 0, 2), ("adv", 1, 0, 3, 1), ("adv", 1, 0, 1, 0),
-    ("adv", 1, 0, 2, 1), ("adv", 1, 0, 3, 0), ("adv", 1, 0, 2, 0), ("xb", 0), ("ya",), ("xb", 1), ("yb",), ("conv", 2, 0), ("conv", 2, 1),
-    ("adv", 2, 0, 0, 0), ("adv", 2, 0, 1, 1), ("adv", 2, 0, 0, 1), ("adv", 2, 0, 2, 1), ("adv", 2, 0, 1, 0), ("zo", 2, 0),
-    ("adv", 2, 0, 2, 0), ("zw", 2, 0), ("cs", 2, 0), ("adv", 2, 0, 3, 0), ("zo", 2, 1), ("adv", 2, 0, 3, 1), ("zo", 2, 2),
-    ("rs1", 2, 0), ("zw", 2, 1), ("zo", 2, 3), ("cs", 2, 1), ("zw", 2, 2), ("zw", 2, 3), ("cs", 2, 2), ("rs2", 2, 0),
-    ("cs", 2, 3), ("rs1", 2, 1), ("rs1", 2, 2), ("rs1", 2, 3), ("rs2", 2, 1), ("tx", 0), ("rs2", 2, 2), ("rs2", 2, 3), ("tx", 1),
-    ("ty", 0), ("ty", 1), ("tg", 0), ("tg", 1), ("th", 0), ("th", 1), ("ti", 0), ("ti", 1), ("tp", 0), ("tp", 1),
+    ("conv", 0, 0), ("conv", 0, 1), ("adv", 0, 0, 0, 0), ("adv", 0, 0, 0, 1), ("adv", 0, 0, 1, 0), ("adv", 0, 0, 1, 1),
+    ("adv", 0, 0, 2, 0), ("adv", 0, 0, 2, 1), ("adv", 0, 0, 3, 0), ("adv", 0, 0, 3, 1), ("zo", 0, 0), ("zw", 0, 0), ("zo", 0, 1),
+    ("zw", 0, 1), ("cs", 0, 0), ("zo", 0, 2), ("zw", 0, 2), ("cs", 0, 1), ("zo", 0, 3), ("zw", 0, 3), ("cs", 0, 2), ("rs1", 0, 0),
+    ("cs", 0, 3), ("rs1", 0, 1), ("rs1", 0, 2), ("rs2", 0, 0), ("rs1", 0, 3), ("rs2", 0, 1), ("rs2", 0, 2), ("ag1", 0, 0),
+    ("rs2", 0, 3), ("ag1", 0, 1), ("ag1", 0, 2), ("ag2", 0, 0), ("zbw", 0, 0), ("ag1", 0, 3), ("zbo", 0, 0), ("ag2", 0, 1),
+    ("zbw", 0, 1), ("adv", 1, 0, 0, 1), ("ag2", 0, 2), ("zbw", 0, 2), ("zbo", 0, 1), ("ag2", 0, 3), ("zbw", 0, 3), ("zbo", 0, 2),
+    ("adv", 1, 0, 0, 0), ("adv", 1, 0, 1, 1), ("zbo", 0, 3), ("adv", 1, 0, 2, 1), ("adv", 1, 0, 1, 0), ("adv", 1, 0, 3, 1),
+    ("adv", 1, 0, 2, 0), ("adv", 1, 0, 3, 0), ("xb", 0), ("ya",), ("xb", 1), ("yb",), ("conv", 2, 0), ("conv", 2, 1), ("adv", 2, 0, 0, 0),
+    ("adv", 2, 0, 0, 1), ("adv", 2, 0, 1, 0), ("adv", 2, 0, 1, 1), ("adv", 2, 0, 2, 0), ("adv", 2, 0, 2, 1), ("adv", 2, 0, 3, 0),
+    ("adv", 2, 0, 3, 1), ("zo", 2, 0), ("zw", 2, 0), ("zo", 2, 1), ("zw", 2, 1), ("cs", 2, 0), ("zo", 2, 2), ("zw", 2, 2),
+    ("cs", 2, 1), ("zo", 2, 3), ("zw", 2, 3), ("cs", 2, 2), ("rs1", 2, 0), ("cs", 2, 3), ("rs1", 2, 1), ("rs1", 2, 2),
+    ("rs2", 2, 0), ("rs1", 2, 3), ("rs2", 2, 1), ("tx", 0), ("rs2", 2, 2), ("rs2", 2, 3), ("tx", 1), ("ty", 0), ("ty", 1),
+    ("tg", 0), ("tg", 1), ("th", 0), ("th", 1), ("ti", 0), ("ti", 1), ("tp", 0), ("tp", 1),
 )
 
 

time: 181 us -> 188 us (1.039)
  Pallas kernels: 175 us -> 182 us
    pallas_call x1, Pallas kernels: 175 us -> 182 us  [local(): pl.pallas_call(body, out_shape=[jax.ShapeDtypeStruct((8, 2, 64, 512), F32...]
where the time goes in v6:
time: 188 us
  Pallas kernels  182 us (97%)
  local copies, waits for them, and re-layouts  4.55 us (2%)
    pallas_call x1, Pallas kernels, local(): pl.pallas_call(body, out_shape=[jax.ShapeDtypeStruct((8, 2, 64, 512), F32...  182 us
    unnamed x4, local copies, waits for them, and re-layouts  4.55 us

profile of v6, /device:TPU:1, one launch (start us, length us, event | category | flops | bytes accessed | tf_op | source)
XLA Modules:
  0.0 187.6 jit_solution(18377802846747387569)
XLA Ops:
  1.3 181.8 %sinkhorn.1 = (f32[8,2,64,512]{3,2,1,0:T(8,128)}, f32[1024,512]{1,0:T(8,128)}) custom-call(f32[1024,512]{1,0:T(8,128)} %bitcast.3, f32[1]{0:T(128)S(6)} %copy.7.wt_ref, f32[3]{0:T(128)} %spread_ref.1), custom_call_target="tpu_custom_call" | custom-call | tf_op jit(solution)/shard_map/sinkhorn/pallas_call | solution.py:499
  183.1 0.0 copy-start
  183.1 3.2 %copy.8 = f32[2,512,512]{2,1,0:T(8,128)} copy(f32[2,512,512]{2,1,0:T(8,128)} %bitcast.5) | data formatting | bytes 4194304
  186.3 0.0 copy-done
  186.3 1.3 copy.9
Async XLA Ops:
  183.1 3.2 %copy-start = (f32[1024,512]{1,0:T(8,128)S(1)}, f32[1024,512]{1,0:T(8,128)}, u32[]{:S(2)}) copy-start(f32[1024,512]{1,0:T(8,128)} %get-tuple-element.5) | copy-start | bytes 6291460

commit v7 on v5

--- a/solution.py
+++ b/solution.py
@@ -24,17 +24,17 @@
 
 ORDER = (
     ("conv", 0, 0), ("conv", 0, 1), ("adv", 0, 0, 0, 0), ("adv", 0, 0, 1, 1), ("adv", 0, 0, 0, 1), ("adv", 0, 0, 2, 0),
-    ("adv", 0, 0, 1, 0), ("zo", 0, 0), ("adv", 0, 0, 2, 1), ("zw", 0, 0), ("cs", 0, 0), ("adv", 0, 0, 3, 0), ("zo", 0, 1),
-    ("adv", 0, 0, 3, 1), ("zw", 0, 2), ("rs1", 0, 0), ("zw", 0, 1), ("zo", 0, 3), ("cs", 0, 1), ("zo", 0, 2), ("zw", 0, 3),
-    ("rs2", 0, 0), ("cs", 0, 3), ("cs", 0, 2), ("rs1", 0, 1), ("ag1", 0, 0), ("rs1", 0, 3), ("rs1", 0, 2), ("rs2", 0, 1),
-    ("ag2", 0, 0), ("zbw", 0, 0), ("rs2", 0, 3), ("rs2", 0, 2), ("zbo", 0, 0), ("ag1", 0, 1), ("ag1", 0, 3), ("adv", 1, 0, 0, 1),
-    ("ag1", 0, 2), ("adv", 1, 0, 0, 0), ("ag2", 0, 1), ("zbw", 0, 1), ("ag2", 0, 3), ("zbw", 0, 3), ("zbo", 0, 1), ("ag2", 0, 2),
-    ("zbw", 0, 2), ("zbo", 0, 3), ("adv", 1, 0, 1, 1), ("zbo", 0, 2), ("adv", 1, 0, 3, 1), ("adv", 1, 0, 1, 0),
-    ("adv", 1, 0, 2, 1), ("adv", 1, 0, 3, 0), ("adv", 1, 0, 2, 0), ("xb", 0), ("ya",), ("xb", 1), ("yb",), ("conv", 2, 0), ("conv", 2, 1),
-    ("adv", 2, 0, 0, 0), ("adv", 2, 0, 1, 1), ("adv", 2, 0, 0, 1), ("adv", 2, 0, 2, 1), ("adv", 2, 0, 1, 0), ("zo", 2, 0),
-    ("adv", 2, 0, 2, 0), ("zw", 2, 0), ("cs", 2, 0), ("adv", 2, 0, 3, 0), ("zo", 2, 1), ("adv", 2, 0, 3, 1), ("zo", 2, 2),
-    ("rs1", 2, 0), ("zw", 2, 1), ("zo", 2, 3), ("cs", 2, 1), ("zw", 2, 2), ("zw", 2, 3), ("cs", 2, 2), ("rs2", 2, 0),
-    ("cs", 2, 3), ("rs1", 2, 1), ("rs1", 2, 2), ("rs1", 2, 3), ("rs2", 2, 1), ("tx", 0), ("rs2", 2, 2), ("rs2", 2, 3), ("tx", 1),
+    ("adv", 0, 0, 1, 0), ("zo", 0, 0), ("adv", 0, 0, 2, 1), ("zw", 0, 0), ("adv", 0, 0, 3, 0), ("cs", 0, 0), ("zo", 0, 1),
+    ("adv", 0, 0, 3, 1), ("zw", 0, 2), ("zw", 0, 1), ("cs", 0, 1), ("zo", 0, 3), ("rs1", 0, 0), ("zo", 0, 2), ("zw", 0, 3),
+    ("cs", 0, 3), ("rs1", 0, 1), ("cs", 0, 2), ("rs2", 0, 0), ("rs1", 0, 3), ("rs2", 0, 1), ("rs1", 0, 2), ("ag1", 0, 0),
+    ("rs2", 0, 3), ("ag1", 0, 1), ("rs2", 0, 2), ("ag2", 0, 0), ("zbw", 0, 0), ("ag1", 0, 3), ("ag2", 0, 1), ("zbw", 0, 1),
+    ("zbo", 0, 0), ("ag1", 0, 2), ("adv", 1, 0, 0, 1), ("ag2", 0, 3), ("zbw", 0, 3), ("zbo", 0, 1), ("adv", 1, 0, 1, 1),
+    ("ag2", 0, 2), ("zbw", 0, 2), ("zbo", 0, 3), ("adv", 1, 0, 0, 0), ("zbo", 0, 2), ("adv", 1, 0, 1, 0), ("adv", 1, 0, 3, 1),
+    ("adv", 1, 0, 3, 0), ("adv", 1, 0, 2, 1), ("adv", 1, 0, 2, 0), ("xb", 0), ("ya",), ("xb", 1), ("yb",), ("conv", 2, 0),
+    ("conv", 2, 1), ("adv", 2, 0, 0, 0), ("adv", 2, 0, 1, 1), ("adv", 2, 0, 0, 1), ("adv", 2, 0, 2, 1), ("adv", 2, 0, 1, 0),
+    ("zo", 2, 0), ("adv", 2, 0, 2, 0), ("zw", 2, 0), ("adv", 2, 0, 3, 0), ("cs", 2, 0), ("zo", 2, 1), ("adv", 2, 0, 3, 1),
+    ("zo", 2, 2), ("zw", 2, 1), ("cs", 2, 1), ("zo", 2, 3), ("rs1", 2, 0), ("zw", 2, 2), ("cs", 2, 2), ("zw", 2, 3), ("cs", 2, 3),
+    ("rs1", 2, 1), ("rs2", 2, 0), ("rs1", 2, 2), ("rs1", 2, 3), ("rs2", 2, 1), ("tx", 0), ("rs2", 2, 2), ("rs2", 2, 3), ("tx", 1),
     ("ty", 0), ("ty", 1), ("tg", 0), ("tg", 1), ("th", 0), ("th", 1), ("ti", 0), ("ti", 1), ("tp", 0), ("tp", 1),
 )
 

time: 181 us -> 183 us (1.011)
  Pallas kernels: 175 us -> 177 us
where the time goes in v7:
time: 183 us
  Pallas kernels  177 us (97%)
  local copies, waits for them, and re-layouts  4.55 us (2%)
    pallas_call x1, Pallas kernels, local(): pl.pallas_call(body, out_shape=[jax.ShapeDtypeStruct((8, 2, 64, 512), F32...  177 us
    unnamed x4, local copies, waits for them, and re-layouts  4.55 us

profile of v7, /device:TPU:1, one launch (start us, length us, event | category | flops | bytes accessed | tf_op | source)
XLA Modules:
  0.0 182.6 jit_solution(18112781474490684540)
XLA Ops:
  1.3 176.8 %sinkhorn.1 = (f32[8,2,64,512]{3,2,1,0:T(8,128)}, f32[1024,512]{1,0:T(8,128)}) custom-call(f32[1024,512]{1,0:T(8,128)} %bitcast.3, f32[1]{0:T(128)S(6)} %copy.7.wt_ref, f32[3]{0:T(128)} %spread_ref.1), custom_call_target="tpu_custom_call" | custom-call | tf_op jit(solution)/shard_map/sinkhorn/pallas_call | solution.py:499
  178.1 0.0 copy-start
  178.1 3.2 %copy.8 = f32[2,512,512]{2,1,0:T(8,128)} copy(f32[2,512,512]{2,1,0:T(8,128)} %bitcast.5) | data formatting | bytes 4194304
  181.3 0.0 copy-done
  181.3 1.3 copy.9
Async XLA Ops:
  178.1 3.2 %copy-start = (f32[1024,512]{1,0:T(8,128)S(1)}, f32[1024,512]{1,0:T(8,128)}, u32[]{:S(2)}) copy-start(f32[1024,512]{1,0:T(8,128)} %get-tuple-element.5) | copy-start | bytes 6291460
